TPU v7x, 256 devices: a whole 4x4x8 slice. The times are simulated.
256 devices in a mesh: seq: 16 (over y, x_lo, core), rep: 16 (over x_hi, z).
Axes of the slice: x: 4 (x_hi: 2, x_lo: 2; x = x_hi * 2 + x_lo), y: 4, z: 8, core: 2. Of those that a mesh axis runs over, the one named last changes fastest.
Arguments:
- queries: bfloat16 [16, 4096, 16, 128], P('rep', 'seq'), may hold values from -12 to 12
- keys: bfloat16 [16, 4096, 16, 128], P('rep', 'seq'), may hold values from -6 to 6
- values: bfloat16 [16, 4096, 16, 128], P('rep', 'seq'), may hold values from -6 to 6
- w_proj: bfloat16 [2048, 512], replicated, may hold values from -0.25 to 0.25
- norm_gain: float32 [512], replicated, may hold values from 0.5 to 1.5
- norm_bias: float32 [512], replicated, may hold values from -3 to 3
- conv_weight: bfloat16 [3, 3, 3, 512, 512], P(None, None, None, None, 'rep'), may hold values from -0.0546875 to 0.0546875
- conv_bias: float32 [512], P('rep'), may hold values from -3 to 3
Outputs:
- decoded: bfloat16 [16, 16, 4, 8, 8, 512], P(None, 'seq', None, None, None, 'rep')
All inputs are finite; a program needn't handle non-finite values.
Results may differ from a plain program's by a relative error of at most 0.0059.
Values may be sent and summed in bfloat16 or wider, within the bound.
A program may use at most 128 MiB of HBM per device.

v0:
```python
import math

import jax
import jax.numpy as jnp
from jax import lax
from jax.experimental import pallas as pl
from jax.experimental.pallas import tpu as pltpu
from jax.sharding import PartitionSpec as P

GROUPS = 32
FRAMES = 4
TH = 8
TW = 8
TILES = 4
HD = 128
N = 16
Z = 8
TOK = 256
LEN = N * TOK
C = 512
CO = C // N
HALF = CO // 2
TAPS = 27
PLANE = 9 * C
DEPTH = TAPS * C + 128
BQ = 512
BK = 512
EXTRA = 16
STEPS = LEN // BQ
PITCH = 24
BF = jnp.bfloat16
F32 = jnp.float32
MESH = pl.DeviceIdType.MESH
RIMS = ((1, 1, 0), (0, -1, 0), (3, 0, 1), (2, 0, -1), (1, 1, 1), (1, 1, -1), (0, -1, 1), (0, -1, -1))


def unit_kernel(
    q_ref, k_ref, v_ref, taps_ref, wp_ref, gain_ref, shift_ref, bias_ref, out_ref,
    q_raw, k_raw, v_raw, by_token, q_out, k_out, v_out,
    q_all, k_all, v_all, v_t, s_even, s_odd, m_buf, o_buf, att,
    w_all, lat, by_lanes, lat_t, edges, rims, stat, stats, field, x_t, out_t, gathered,
    q_send, q_recv, k_send, k_recv, v_send, v_recv, o_send, o_recv,
    raw_in, w_own, w_send, w_recv, c_send, c_recv, e_send, e_recv, t_send, t_recv, y_send, y_recv,
):
    me = lax.axis_index("seq")
    rep = lax.axis_index("rep")
    x_hi = rep // Z
    z = lax.rem(rep, Z)
    half = lax.rem(me, 2)
    other_core = me + 1 - 2 * half
    beside = {
        "seq": me + 2 - 4 * lax.rem(me // 2, 2),
        "rep": lax.rem(rep + Z, N),
    }

    barrier = pltpu.get_barrier_semaphore()

    def greet(t, carry):
        pl.semaphore_signal(
            barrier, inc=1, device_id={"seq": lax.rem(me + t, N)}, device_id_type=MESH
        )
        pl.semaphore_signal(
            barrier, inc=1, device_id={"rep": lax.rem(rep + t, N)}, device_id_type=MESH
        )
        return carry

    lax.fori_loop(1, N, greet, 0)
    pl.semaphore_signal(barrier, inc=1, device_id=beside, device_id_type=MESH)

    k_in = pltpu.make_async_copy(k_ref, k_raw, raw_in.at[0])
    v_in = pltpu.make_async_copy(v_ref, v_raw, raw_in.at[1])
    q_in = pltpu.make_async_copy(q_ref, q_raw, raw_in.at[2])
    k_in.start()
    v_in.start()
    q_in.start()

    def ds(start, size):
        return pl.ds(pl.multiple_of(start, size), size)

    def own_tap(t):
        return pltpu.make_async_copy(
            taps_ref.at[t], w_all.at[ds(rep * CO, CO), ds(t * C, C)], w_own.at[t]
        )

    def tap_start(t, carry):
        own_tap(t).start()
        return carry

    lax.fori_loop(0, TAPS, tap_start, 0)
    square = (CO, CO)
    on = lax.broadcasted_iota(jnp.int32, square, 0) == lax.broadcasted_iota(jnp.int32, square, 1)
    bias = jnp.sum(
        jnp.where(on, jnp.broadcast_to(bias_ref[...], square), 0.0), axis=1, keepdims=True
    )
    high = bias.astype(BF).astype(F32)
    middle = (bias - high).astype(BF).astype(F32)
    low = bias - high - middle
    lane = lax.broadcasted_iota(jnp.int32, (CO, HD), 1)
    nought = jnp.zeros((CO, HD), F32)
    parts = jnp.where(lane == 0, high, jnp.where(lane == 1, middle, jnp.where(lane == 2, low, nought)))
    w_all[ds(rep * CO, CO), TAPS * C :] = parts.astype(BF)
    v_t[HD:] = jnp.ones((EXTRA, LEN), BF)

    def by_head(copy, raw, out):
        copy.wait()

        def widen(b, carry):
            by_token[ds(b * TOK, TOK)] = raw[ds(b * TOK, TOK)].astype(F32)
            return carry

        lax.fori_loop(0, N, widen, 0)
        for h in range(N):
            out[h] = by_token[pl.ds(h, TOK, stride=N)].astype(BF)

    by_head(k_in, k_raw, k_out)
    pl.semaphore_wait(barrier, 2 * (N - 1) + 1)

    def k_copy(t):
        to = lax.rem(me + t, N)
        return pltpu.make_async_remote_copy(
            src_ref=k_out.at[to], dst_ref=k_all.at[ds(me * TOK, TOK), pl.ds(0, HD)],
            send_sem=k_send.at[t], recv_sem=k_recv.at[t],
            device_id={"seq": to}, device_id_type=MESH,
        )

    def v_copy(t):
        to = lax.rem(me + t, N)
        return pltpu.make_async_remote_copy(
            src_ref=v_out.at[to], dst_ref=v_all.at[ds(me * TOK, TOK)],
            send_sem=v_send.at[t], recv_sem=v_recv.at[t],
            device_id={"seq": to}, device_id_type=MESH,
        )

    def q_copy(t):
        to = lax.rem(me - t + N, N)
        return pltpu.make_async_remote_copy(
            src_ref=q_out.at[to], dst_ref=q_all.at[ds(t * TOK, TOK)],
            send_sem=q_send.at[t], recv_sem=q_recv.at[t],
            device_id={"seq": to}, device_id_type=MESH,
        )

    def o_copy(t):
        to = lax.rem(me + t, N)
        return pltpu.make_async_remote_copy(
            src_ref=o_buf.at[ds(t * TOK, TOK)], dst_ref=att.at[:, ds(me * HD, HD)],
            send_sem=o_send.at[t], recv_sem=o_recv.at[t],
            device_id={"seq": to}, device_id_type=MESH,
        )

    def every(act, copy, first=1, last=N):
        def body(t, carry):
            getattr(copy(t), act)()
            return carry
        lax.fori_loop(first, last, body, 0)

    pieces = (
        [(0, -d, "up") for d in (1, 2, 3, 4)] + [(0, d, "down") for d in (1, 2, 3)]
        + [(1, d, "across") for d in (0, -1, -2, -3, 3, 4)] + [(1, d, "down") for d in (1, 2)]
    )

    def shard_rows(x, d):
        at_x = 1 - x_hi if x else x_hi
        return ds((at_x * Z + lax.rem(z + d + Z, Z)) * CO + half * HALF, HALF)

    def w_copy(i):
        x, d, way = pieces[i]
        if way == "across":
            held, to = shard_rows(0, d), beside
        else:
            turn = 1 if way == "up" else -1
            held = shard_rows(x, d + turn)
            to = {"rep": x_hi * Z + lax.rem(z + turn + Z, Z)}
        return pltpu.make_async_remote_copy(
            src_ref=w_all.at[held], dst_ref=w_all.at[held],
            send_sem=w_send.at[i], recv_sem=w_recv.at[i],
            device_id=to, device_id_type=MESH,
        )

    def core_copy(i):
        x, d, _ = pieces[i]
        held = shard_rows(x, d)
        return pltpu.make_async_remote_copy(
            src_ref=w_all.at[held], dst_ref=w_all.at[held],
            send_sem=c_send.at[i], recv_sem=c_recv.at[i],
            device_id={"seq": other_core}, device_id_type=MESH,
        )

    def relay(i, *onward):
        w_copy(i).wait_recv()
        for j in onward:
            w_copy(j).start()
        core_copy(i).start()

    every("start", k_copy)
    every("wait", own_tap, 0, TAPS)
    w_copy(0).start()
    w_copy(4).start()
    w_copy(7).start()
    by_head(v_in, v_raw, v_out)
    every("start", v_copy)
    by_head(q_in, q_raw, q_out)
    every("start", q_copy)

    def twice(place, block):
        k_all[place, HD:] = block

    def flip(place, block):
        v_t[:HD, place] = jnp.transpose(block)

    mine = ds(me * TOK, TOK)
    k_all[mine, :HD] = k_out[me]
    twice(mine, k_out[me])
    flip(mine, v_out[me])
    q_all[:TOK] = q_out[me]

    def k_arrive(t, carry):
        k_copy(t).wait_recv()
        place = ds(lax.rem(me - t + N, N) * TOK, TOK)
        twice(place, k_all[place, :HD])
        return carry

    lax.fori_loop(1, N, k_arrive, 0)

    factor = HD ** (-0.5) * math.log2(math.e)

    def query_pair(u):
        wide = q_all[ds(u * BQ, BQ)].astype(F32) * factor
        first = wide.astype(BF)
        rest = (wide - first.astype(F32)).astype(BF)
        return jnp.concatenate([jnp.transpose(first), jnp.transpose(rest)], axis=0)

    def scores(pair, s_buf, c, top):
        keys = pl.ds(c * BK, BK)
        s = jnp.dot(k_all[keys], pair, preferred_element_type=F32)
        s_buf[keys] = s
        part = jnp.max(s.reshape(BK // 8, 8, BQ), axis=0)
        return part if top is None else jnp.maximum(top, part)

    def settle(top):
        m_buf[...] = jnp.broadcast_to(jnp.max(top, axis=0, keepdims=True), (8, BQ))

    def weigh(s_buf, c, m, total):
        keys = pl.ds(c * BK, BK)
        p = jnp.exp2(s_buf[keys].reshape(BK // 8, 8, BQ) - m[None]).reshape(BK, BQ).astype(BF)
        got = jnp.dot(v_t[:, keys], p, preferred_element_type=F32)
        return got if total is None else total + got

    def emit(u, total):
        o = (total[:HD] / total[HD : HD + 1]).astype(BF)
        o_buf[ds(u * BQ, BQ)] = jnp.transpose(o)

    def step(u, now, then):
        if then is not None:
            q_copy(2 * u + 2).wait_recv()
            q_copy(2 * u + 3).wait_recv()
            pair = query_pair(u + 1)
        m = m_buf[...]
        top = None
        total = None
        for c in range(LEN // BK):
            if then is not None:
                top = scores(pair, then, c, top)
            total = weigh(now, c, m, total)
        if then is not None:
            settle(top)
        emit(u, total)

    q_copy(1).wait_recv()
    pair = query_pair(0)
    top = None
    for c in range(LEN // BK):
        top = scores(pair, s_even, c, top)
    settle(top)
    relay(0, 1, 8)
    relay(4, 5)
    relay(7, 13)

    def v_arrive(t, carry):
        v_copy(t).wait_recv()
        place = ds(lax.rem(me - t + N, N) * TOK, TOK)
        flip(place, v_all[place])
        return carry

    lax.fori_loop(1, N, v_arrive, 0)
    relay(1, 2, 9)
    relay(5, 6)
    relay(8)

    def steps(i, carry):
        step(2 * i, s_even, s_odd)

        @pl.when(i > 0)
        def _():
            o_copy(4 * i).start()

        o_copy(4 * i + 1).start()

        step(2 * i + 1, s_odd, s_even)
        o_copy(4 * i + 2).start()
        o_copy(4 * i + 3).start()

        @pl.when(i == 0)
        def _():
            relay(2, 3, 10)
            relay(6, 11)
            relay(9)

        @pl.when(i == 1)
        def _():
            relay(3, 12)
            relay(13, 14)
            relay(10)

        @pl.when(i == 2)
        def _():
            relay(11)
            relay(14)

        return carry

    lax.fori_loop(0, STEPS // 2 - 1, steps, 0)
    step(STEPS - 2, s_even, s_odd)
    o_copy(N - 4).start()
    o_copy(N - 3).start()
    step(STEPS - 1, s_odd, None)
    o_copy(N - 2).start()
    o_copy(N - 1).start()
    own_o = pltpu.make_async_copy(o_buf.at[pl.ds(0, TOK)], att.at[:, ds(me * HD, HD)], o_recv.at[0])
    own_o.start()
    every("wait_send", k_copy)
    every("wait_send", v_copy)
    every("wait_send", q_copy)
    own_o.wait()
    every("wait_recv", o_copy)

    latent = jnp.dot(att[...], wp_ref[...], preferred_element_type=F32).astype(BF)
    wide = latent.astype(F32)
    lat[...] = wide
    for f in range(FRAMES):
        at = pl.ds(f * TW, TW)
        edges[0, at] = lat[pl.ds(f * TH * TW, TW)].astype(BF)
        edges[1, at] = lat[pl.ds((f + 1) * TH * TW - TW, TW)].astype(BF)
    for j in range(C // HD):
        lanes = pl.ds(j * HD, HD)
        by_lanes[j] = wide[:, j * HD : (j + 1) * HD]
        edges[2, :, lanes] = by_lanes[j, pl.ds(0, FRAMES * TH, stride=TW)].astype(BF)
        edges[3, :, lanes] = by_lanes[j, pl.ds(TW - 1, FRAMES * TH, stride=TW)].astype(BF)

    row, column = me // TILES, lax.rem(me, TILES)

    def rim_copy(n):
        edge, down, right = RIMS[n]
        to = lax.rem(row + down + TILES, TILES) * TILES + lax.rem(column + right + TILES, TILES)
        return pltpu.make_async_remote_copy(
            src_ref=edges.at[edge], dst_ref=rims.at[n],
            send_sem=e_send.at[n], recv_sem=e_recv.at[n],
            device_id={"seq": to}, device_id_type=MESH,
        )

    for n in range(len(RIMS)):
        rim_copy(n).start()

    line = lax.broadcasted_iota(jnp.int32, (8, C), 0)
    sums = jnp.where(
        line == 0,
        jnp.sum(wide, axis=0, keepdims=True),
        jnp.where(line == 1, jnp.sum(wide * wide, axis=0, keepdims=True), 0.0),
    )
    size = C // GROUPS
    member = lax.broadcasted_iota(jnp.int32, (C, HD), 0) // size
    into = (member == lax.broadcasted_iota(jnp.int32, (C, HD), 1)).astype(F32)
    stat[...] = jnp.dot(
        sums, into, precision=lax.Precision.HIGHEST, preferred_element_type=F32
    )

    def stat_copy(t):
        return pltpu.make_async_remote_copy(
            src_ref=stat, dst_ref=stats.at[me],
            send_sem=t_send.at[t], recv_sem=t_recv.at[t],
            device_id={"seq": lax.rem(me + t, N)}, device_id_type=MESH,
        )

    every("start", stat_copy)
    stats[me] = stat[...]
    lat_t[...] = jnp.transpose(latent)
    x_t[PLANE:] = jnp.where(
        lax.broadcasted_iota(jnp.int32, (128, TOK), 0) < 3, 1.0, 0.0
    ).astype(BF)
    every("wait_recv", stat_copy)

    total = jnp.sum(stats[...], axis=0) / (LEN * size)
    mean = total[0:1]
    var = total[1:2] - mean * mean
    pick = lax.broadcasted_iota(jnp.int32, (8, HD), 0)
    both = jnp.where(pick == 0, mean, jnp.where(pick == 1, lax.rsqrt(var + 1e-06), 0.0))
    member = lax.broadcasted_iota(jnp.int32, (HD, C), 1) // size
    out_of = (member == lax.broadcasted_iota(jnp.int32, (HD, C), 0)).astype(F32)
    both = jnp.dot(both, out_of, precision=lax.Precision.HIGHEST, preferred_element_type=F32)
    mean, inverse = both[0:1], both[1:2]
    gain, shift = gain_ref[...], shift_ref[...]

    def activate(x):
        return jax.nn.silu((x - mean) * inverse * gain + shift)

    inner = activate(lat[...])
    for f in range(FRAMES):
        for h in range(TH):
            place = (f * (TH + 2) + 1 + h) * PITCH + 8
            field[pl.ds(place, TW)] = inner[(f * TH + h) * TW : (f * TH + h + 1) * TW]

    above, below = row > 0, row < TILES - 1
    before, after = column > 0, column < TILES - 1
    inside = (
        above, below, before, after,
        above & before, above & after, below & before, below & after,
    )
    for n in range(len(RIMS)):
        rim_copy(n).wait_recv()
        rim = jnp.where(inside[n], activate(rims[n].astype(F32)), 0.0)
        for f in range(FRAMES):
            mine = rim[f * TW : (f + 1) * TW]
            first = f * (TH + 2) * PITCH
            last = first + (TH + 1) * PITCH
            if n == 0:
                field[pl.ds(first + 8, TW)] = mine
            elif n == 1:
                field[pl.ds(last + 8, TW)] = mine
            elif n == 2:
                for h in range(TH):
                    field[pl.ds(first + (h + 1) * PITCH + 7, 1)] = mine[h : h + 1]
            elif n == 3:
                for h in range(TH):
                    field[pl.ds(first + (h + 1) * PITCH + 16, 1)] = mine[h : h + 1]
            elif n == 4:
                field[pl.ds(first + 7, 1)] = mine[TW - 1 :]
            elif n == 5:
                field[pl.ds(first + 16, 1)] = mine[:1]
            elif n == 6:
                field[pl.ds(last + 7, 1)] = mine[TW - 1 :]
            else:
                field[pl.ds(last + 16, 1)] = mine[:1]

    for r in range(3):
        for s in range(3):
            window = jnp.concatenate(
                [
                    field[pl.ds((f * (TH + 2) + r + h) * PITCH + 7 + s, TW)]
                    for f in range(FRAMES)
                    for h in range(TH)
                ],
                axis=0,
            )
            x_t[pl.ds((r * 3 + s) * C, C)] = jnp.transpose(window.astype(BF))

    relay(12)
    every_piece = range(len(pieces))
    for i in every_piece:
        core_copy(i).wait_recv()

    now = jnp.dot(w_all[:, 2 * PLANE :], x_t[...], preferred_element_type=F32)
    one = jnp.dot(w_all[:, PLANE : 2 * PLANE], x_t[:PLANE], preferred_element_type=F32)
    two = jnp.dot(w_all[:, :PLANE], x_t[:PLANE, : TOK // 2], preferred_element_type=F32)
    at = lax.broadcasted_iota(jnp.int32, (C, TOK), 1)
    frame = TH * TW
    one = jnp.where(at >= frame, pltpu.roll(one, frame, 1), 0.0)
    two = jnp.concatenate([jnp.zeros((C, TOK // 2), F32), two], axis=1)
    out_t[...] = (lat_t[...].astype(F32) + now + one + two).astype(BF)

    def y_copy(t):
        to = lax.rem(rep + t, N)
        return pltpu.make_async_remote_copy(
            src_ref=out_t.at[ds(to * CO, CO)], dst_ref=gathered.at[rep],
            send_sem=y_send.at[t], recv_sem=y_recv.at[t],
            device_id={"rep": to}, device_id_type=MESH,
        )

    every("start", y_copy)
    gathered[rep] = out_t[ds(rep * CO, CO)]
    for i in every_piece:
        w_copy(i).wait_send()
        core_copy(i).wait_send()
    for n in range(len(RIMS)):
        rim_copy(n).wait_send()
    every("wait_send", o_copy)
    every("wait_send", stat_copy)
    every("wait_recv", y_copy)
    out_ref[...] = gathered[...]
    every("wait_send", y_copy)


def unit(q, k, v, taps, w_proj, gain, shift, bias):
    sem = pltpu.SemaphoreType.DMA
    vmem = pl.BlockSpec(memory_space=pltpu.VMEM)
    return pl.pallas_call(
        unit_kernel,
        out_shape=jax.ShapeDtypeStruct((N, CO, TOK), BF),
        in_specs=[pl.BlockSpec(memory_space=pl.ANY)] * 4 + [vmem] * 4,
        out_specs=vmem,
        scratch_shapes=[
            pltpu.VMEM((LEN, HD), BF),
            pltpu.VMEM((LEN, HD), BF),
            pltpu.VMEM((LEN, HD), BF),
            pltpu.VMEM((LEN, HD), F32),
            pltpu.VMEM((N, TOK, HD), BF),
            pltpu.VMEM((N, TOK, HD), BF),
            pltpu.VMEM((N, TOK, HD), BF),
            pltpu.VMEM((LEN, HD), BF),
            pltpu.VMEM((LEN, 2 * HD), BF),
            pltpu.VMEM((LEN, HD), BF),
            pltpu.VMEM((HD + EXTRA, LEN), BF),
            pltpu.VMEM((LEN, BQ), F32),
            pltpu.VMEM((LEN, BQ), F32),
            pltpu.VMEM((8, BQ), F32),
            pltpu.VMEM((LEN, HD), BF),
            pltpu.VMEM((TOK, N * HD), BF),
            pltpu.VMEM((C, DEPTH), BF),
            pltpu.VMEM((TOK, C), F32),
            pltpu.VMEM((C // HD, TOK, HD), F32),
            pltpu.VMEM((C, TOK), BF),
            pltpu.VMEM((4, FRAMES * TW, C), BF),
            pltpu.VMEM((len(RIMS), FRAMES * TW, C), BF),
            pltpu.VMEM((8, HD), F32),
            pltpu.VMEM((N, 8, HD), F32),
            pltpu.VMEM((FRAMES * (TH + 2) * PITCH, C), F32),
            pltpu.VMEM((PLANE + 128, TOK), BF),
            pltpu.VMEM((C, TOK), BF),
            pltpu.VMEM((N, CO, TOK), BF),
        ]
        + [sem((N,))] * 8
        + [sem((3,)), sem((TAPS,))]
        + [sem((N,))] * 4
        + [sem((len(RIMS),))] * 2
        + [sem((N,))] * 4,
        compiler_params=pltpu.CompilerParams(
            collective_id=0, has_side_effects=True, vmem_limit_bytes=62 * 2**20
        ),
        cost_estimate=pl.CostEstimate(
            flops=4 * LEN * LEN * HD + 2 * TOK * DEPTH * C,
            bytes_accessed=8 * 2**20,
            transcendentals=LEN * LEN,
        ),
        name="unit",
    )(q, k, v, taps, w_proj, gain, shift, bias)


def shards(queries, keys, values, w_proj, norm_gain, norm_bias, conv_weight, conv_bias):
    taps = conv_weight.reshape(TAPS, C, CO).transpose(0, 2, 1)
    q, k, v = (a.reshape(LEN, HD) for a in (queries, keys, values))
    out = unit(
        q, k, v, taps, w_proj, norm_gain[None], norm_bias[None], conv_bias[None]
    )
    return out.transpose(0, 2, 1).reshape(N, 1, FRAMES, TH, TW, CO)


def solution(mesh):
    return jax.shard_map(
        shards,
        mesh=mesh,
        in_specs=(
            P("rep", "seq", None, None),
            P("rep", "seq", None, None),
            P("rep", "seq", None, None),
            P(),
            P(),
            P(),
            P(None, None, None, None, "rep"),
            P("rep"),
        ),
        out_specs=P(None, "seq", None, None, None, "rep"),
        check_vma=False,
    )
```

profile of v0, /device:TPU:2, one launch (start us, length us, event | category | flops | bytes accessed | tf_op | source)
XLA Modules:
  0.0 116.0 jit_solution(645146098706194163)
XLA Ops:
  0.0 113.7 %unit.1 = bf16[16,32,256]{2,1,0:T(8,128)(2,1)} custom-call(bf16[4096,128]{1,0:T(8,128)(2,1)} %bitcast.14, bf16[4096,128]{1,0:T(8,128)(2,1)} %bitcast.15, bf16[4096,128]{1,0:T(8,128)(2,1)} %bitcast.16, bf16[27,32,512]{2,1,0:T(8,128)(2,1)} %bitcast.17, bf16[2048,512]{1,0:T(8,128)(2,1)} %wp_ref.1, f32[1,512]{1,0:T(1,128)} %bitcast.18, f32[1,512]{1,0:T(1,128)} %bitcast.19, ...), custom_call_target="tpu_custom_call" | custom-call | flops 12247367680 | bytes 8388608 | tf_op jit(solution)/shard_map/unit/pallas_call | solution.py:494
  113.7 2.3 %copy.10 = bf16[16,256,32]{2,1,0:T(8,128)(2,1)} copy(bf16[16,256,32]{1,2,0:T(8,128)(2,1)} %bitcast.13) | data formatting | bytes 524288 | tf_op jit(solution)/shard_map/transpose | solution.py:552
where the time goes:
time: 117 us; the launch traced here: 116 us
  Pallas kernels  114 us (97%)
  local copies, waits for them, and re-layouts  2.27 us (2%)
    pallas_call x1, Pallas kernels, unit(): pl.pallas_call(unit_kernel, out_shape=jax.ShapeDtypeStruct((N, CO, TOK),...  114 us

commit v1 on v0

v1 whole, which is shorter than its diff:
```python
import math

import jax
import jax.numpy as jnp
from jax import lax
from jax.experimental import pallas as pl
from jax.experimental.pallas import tpu as pltpu
from jax.sharding import PartitionSpec as P

GROUPS = 32
FRAMES = 4
TH = 8
TW = 8
TILES = 4
HD = 128
N = 16
Z = 8
TOK = 256
LEN = N * TOK
C = 512
CO = C // N
HALF = CO // 2
TAPS = 27
PLANE = 9 * C
DEPTH = TAPS * C + 128
BQ = 512
BK = 512
EXTRA = 16
STEPS = LEN // BQ
PITCH = 24
BF = jnp.bfloat16
F32 = jnp.float32
MESH = pl.DeviceIdType.MESH
CORNERS = 4 * FRAMES * TW
RIMS = (
    (32, 32, 1, 0), (0, 32, -1, 0), (96, 32, 0, 1), (64, 32, 0, -1),
    (CORNERS + 48, 16, 1, 1), (CORNERS + 32, 16, 1, -1), (CORNERS + 16, 16, -1, 1), (CORNERS, 16, -1, -1),
)
RIM_ROWS = CORNERS + 4 * 16
CH = C // 2


def unit_kernel(
    q_ref, k_ref, v_ref, taps_ref, wp_ref, gain_ref, shift_ref, bias_ref, out_ref,
    q_raw, k_raw, v_raw, by_token, q_out, k_out, v_out,
    k_stop, v_stop, q_all, k_all, v_all, v_t, s_even, s_odd, m_buf, q_t, acc, o_buf, att, wp,
    w_all, lat, by_lanes, edges, rims, stat, stats, moments, field, x_t, by_frame, out_t, gathered,
    q_send, q_recv, k_send, k_recv, v_send, v_recv, o_send, o_recv,
    k_stop_send, k_stop_recv, v_stop_send, v_stop_recv,
    raw_in, w_own, w_send, w_recv, c_send, c_recv, e_send, e_recv, t_send, t_recv, b_send, b_recv, y_send, y_recv,
):
    me = lax.axis_index("seq")
    rep = lax.axis_index("rep")
    x_hi = rep // Z
    z = lax.rem(rep, Z)
    half = lax.rem(me, 2)
    other_core = me + 1 - 2 * half
    twin = me + 2 - 4 * lax.rem(me // 2, 2)
    beside = {"seq": twin, "rep": lax.rem(rep + Z, N)}

    def along_z(d):
        return x_hi * Z + lax.rem(z + d + Z, Z)

    barrier = pltpu.get_barrier_semaphore()

    def greet(t, carry):
        pl.semaphore_signal(
            barrier, inc=1, device_id={"seq": lax.rem(me + t, N)}, device_id_type=MESH
        )
        return carry

    def greet_z(t, carry):
        for seq in (me, twin):
            pl.semaphore_signal(
                barrier, inc=1, device_id={"seq": seq, "rep": along_z(t)}, device_id_type=MESH
            )
        return carry

    lax.fori_loop(1, N, greet, 0)
    lax.fori_loop(1, Z, greet_z, 0)
    pl.semaphore_signal(barrier, inc=1, device_id=beside, device_id_type=MESH)

    k_in = pltpu.make_async_copy(k_ref, k_raw, raw_in.at[0])
    v_in = pltpu.make_async_copy(v_ref, v_raw, raw_in.at[1])
    q_in = pltpu.make_async_copy(q_ref, q_raw, raw_in.at[2])
    wp_in = pltpu.make_async_copy(wp_ref, wp, raw_in.at[3])
    k_in.start()
    v_in.start()
    q_in.start()
    wp_in.start()

    def ds(start, size):
        return pl.ds(pl.multiple_of(start, size), size)

    def own_tap(t):
        return pltpu.make_async_copy(
            taps_ref.at[t], w_all.at[ds(z * CO, CO), ds(t * C, C)], w_own.at[t]
        )

    def tap_start(t, carry):
        own_tap(t).start()
        return carry

    lax.fori_loop(0, TAPS, tap_start, 0)
    square = (CO, CO)
    on = lax.broadcasted_iota(jnp.int32, square, 0) == lax.broadcasted_iota(jnp.int32, square, 1)
    bias = jnp.sum(
        jnp.where(on, jnp.broadcast_to(bias_ref[...], square), 0.0), axis=1, keepdims=True
    )
    high = bias.astype(BF).astype(F32)
    middle = (bias - high).astype(BF).astype(F32)
    low = bias - high - middle
    lane = lax.broadcasted_iota(jnp.int32, (CO, HD), 1)
    nought = jnp.zeros((CO, HD), F32)
    parts = jnp.where(lane == 0, high, jnp.where(lane == 1, middle, jnp.where(lane == 2, low, nought)))
    w_all[ds(z * CO, CO), TAPS * C :] = parts.astype(BF)
    v_t[HD:] = jnp.ones((EXTRA, LEN), BF)

    def by_head(copy, raw, out):
        copy.wait()

        def widen(b, carry):
            by_token[ds(b * TOK, TOK)] = raw[ds(b * TOK, TOK)].astype(F32)
            return carry

        lax.fori_loop(0, N, widen, 0)
        for h in range(N):
            out[h] = by_token[pl.ds(h, TOK, stride=N)].astype(BF)

    by_head(k_in, k_raw, k_out)
    pl.semaphore_wait(barrier, N + 2 * (Z - 1))

    band, lo = me // TILES, lax.rem(me // 2, 2)

    def column_of(j):
        return 2 * (lo + j // 2 - 2 * lo * (j // 2)) + half + j % 2 - 2 * half * (j % 2)

    def across_rows(j, rows):
        way = -1 if j < 2 else 1
        return lax.rem(band + way * rows + TILES, TILES) * TILES

    def straight(t):
        row = lax.rem(me + t, N) // TILES
        return lax.rem(row - band + TILES, TILES) != 2

    class Exchange:
        def __init__(self, out, whole, send, recv, stop, stop_send, stop_recv):
            self.out, self.whole, self.send, self.recv = out, whole, send, recv
            self.stop, self.stop_send, self.stop_recv = stop, stop_send, stop_recv

        def copy(self, t):
            to = lax.rem(me + t, N)
            return pltpu.make_async_remote_copy(
                src_ref=self.out.at[to], dst_ref=self.whole.at[ds(me * TOK, TOK)],
                send_sem=self.send.at[t], recv_sem=self.recv.at[t],
                device_id={"seq": to}, device_id_type=MESH,
            )

        def first(self, j):
            to = across_rows(j, 2) + column_of(j)
            t = lax.rem(to - me + N, N)
            return pltpu.make_async_remote_copy(
                src_ref=self.out.at[to], dst_ref=self.stop.at[j],
                send_sem=self.send.at[t], recv_sem=self.stop_recv.at[j],
                device_id={"seq": across_rows(j, 1) + lax.rem(me, TILES)}, device_id_type=MESH,
            )

        def second(self, j):
            to = across_rows(j, 1) + column_of(j)
            origin = across_rows(j, -1) + lax.rem(me, TILES)
            t = lax.rem(to - origin + N, N)
            return pltpu.make_async_remote_copy(
                src_ref=self.stop.at[j], dst_ref=self.whole.at[ds(origin * TOK, TOK)],
                send_sem=self.stop_send.at[j], recv_sem=self.recv.at[t],
                device_id={"seq": to}, device_id_type=MESH,
            )

        def start(self):
            for j in range(4):
                self.first(j).start()

            def body(t, carry):
                @pl.when(straight(t))
                def _():
                    self.copy(t).start()
                return carry

            lax.fori_loop(1, N, body, 0)

        def forward(self):
            for j in range(4):
                self.first(j).wait_recv()
                self.second(j).start()

        def wait_send(self):
            every("wait_send", self.copy)
            for j in range(4):
                self.second(j).wait_send()

    def q_copy(t):
        to = lax.rem(me - t + N, N)
        return pltpu.make_async_remote_copy(
            src_ref=q_out.at[to], dst_ref=q_all.at[ds(t * TOK, TOK)],
            send_sem=q_send.at[t], recv_sem=q_recv.at[t],
            device_id={"seq": to}, device_id_type=MESH,
        )

    def o_copy(t):
        to = lax.rem(me + t, N)
        return pltpu.make_async_remote_copy(
            src_ref=o_buf.at[ds(t * TOK, TOK)], dst_ref=att.at[:, ds(me * HD, HD)],
            send_sem=o_send.at[t], recv_sem=o_recv.at[t],
            device_id={"seq": to}, device_id_type=MESH,
        )

    def every(act, copy, first=1, last=N):
        def body(t, carry):
            getattr(copy(t), act)()
            return carry
        lax.fori_loop(first, last, body, 0)

    k_move = Exchange(k_out, k_all, k_send, k_recv, k_stop, k_stop_send, k_stop_recv)
    v_move = Exchange(v_out, v_all, v_send, v_recv, v_stop, v_stop_send, v_stop_recv)

    pieces = [(-d, 1) for d in (1, 2, 3, 4)] + [(d, -1) for d in (1, 2, 3)]

    def shard_rows(d):
        return ds(lax.rem(z + d + Z, Z) * CO + half * HALF, HALF)

    def w_copy(i):
        d, turn = pieces[i]
        held = shard_rows(d + turn)
        return pltpu.make_async_remote_copy(
            src_ref=w_all.at[held], dst_ref=w_all.at[held],
            send_sem=w_send.at[i], recv_sem=w_recv.at[i],
            device_id={"rep": along_z(turn)}, device_id_type=MESH,
        )

    def core_copy(i):
        held = shard_rows(pieces[i][0])
        return pltpu.make_async_remote_copy(
            src_ref=w_all.at[held], dst_ref=w_all.at[held],
            send_sem=c_send.at[i], recv_sem=c_recv.at[i],
            device_id={"seq": other_core}, device_id_type=MESH,
        )

    def relay(i, *onward):
        w_copy(i).wait_recv()
        for j in onward:
            w_copy(j).start()
        core_copy(i).start()

    k_move.start()
    every("wait", own_tap, 0, TAPS)
    w_copy(0).start()
    w_copy(4).start()
    by_head(v_in, v_raw, v_out)
    by_head(q_in, q_raw, q_out)
    k_move.forward()

    def flip(place, block):
        v_t[:HD, place] = jnp.transpose(block)

    mine = ds(me * TOK, TOK)
    k_all[mine] = k_out[me]
    flip(mine, v_out[me])
    q_all[:TOK] = q_out[me]
    every("wait_recv", k_move.copy)
    v_move.start()
    every("start", q_copy, 1, 4)

    factor = HD ** (-0.5) * math.log2(math.e)

    def query_block(u):
        q_t[...] = jnp.transpose(q_all[ds(u * BQ, BQ)])

    def scores(s_buf, keys, top):
        s = jnp.dot(k_all[keys], q_t[...], preferred_element_type=F32)
        s_buf[keys] = s
        return jnp.maximum(top, jnp.max(s.reshape(BK // 8, 8, BQ), axis=0))

    lowest = jnp.full((8, BQ), -jnp.inf, F32)

    def settle(top):
        m_buf[...] = jnp.broadcast_to(jnp.max(top, axis=0, keepdims=True), (8, BQ))

    def exps(s_buf, keys, m):
        below = s_buf[keys].reshape(BK // 8, 8, BQ) - m[None]
        return jnp.exp2(below * factor).reshape(BK, BQ).astype(BF)

    def weigh(p, keys):
        acc[...] += jnp.dot(v_t[:, keys], p, preferred_element_type=F32)

    def emit(u):
        o = (acc[:HD] / acc[HD : HD + 1]).astype(BF)
        o_buf[ds(u * BQ, BQ)] = jnp.transpose(o)

    def step(u, now, then):
        if then is not None:
            q_copy(2 * u + 2).wait_recv()
            q_copy(2 * u + 3).wait_recv()
            query_block(u + 1)
        m = m_buf[...]
        acc[...] = jnp.zeros_like(acc)

        def chunk(c, top):
            keys = ds(c * BK, BK)
            p = exps(now, keys, m)
            if then is not None:
                top = scores(then, keys, top)
            weigh(p, keys)
            return top

        top = lax.fori_loop(0, LEN // BK, chunk, lowest)
        if then is not None:
            settle(top)
        emit(u)

    q_copy(1).wait_recv()
    query_block(0)
    settle(
        lax.fori_loop(
            0, LEN // BK, lambda c, top: scores(s_even, ds(c * BK, BK), top), lowest
        )
    )
    v_move.forward()
    relay(0, 1)
    relay(4, 5)

    def v_arrive(t, carry):
        v_move.copy(t).wait_recv()
        place = ds(lax.rem(me - t + N, N) * TOK, TOK)
        flip(place, v_all[place])
        return carry

    lax.fori_loop(1, N, v_arrive, 0)
    every("start", q_copy, 4, 8)
    relay(1, 2)
    relay(5, 6)

    def steps(i, carry):
        @pl.when(i < 2)
        def _():
            every("start", q_copy, 8 + 4 * i, 12 + 4 * i)

        step(2 * i, s_even, s_odd)

        @pl.when(i > 0)
        def _():
            o_copy(4 * i).start()

        o_copy(4 * i + 1).start()

        step(2 * i + 1, s_odd, s_even)
        o_copy(4 * i + 2).start()
        o_copy(4 * i + 3).start()

        @pl.when(i == 1)
        def _():
            relay(2, 3)
            relay(6)

        return carry

    lax.fori_loop(0, STEPS // 2 - 1, steps, 0)
    step(STEPS - 2, s_even, s_odd)
    o_copy(N - 4).start()
    o_copy(N - 3).start()
    step(STEPS - 1, s_odd, None)
    o_copy(N - 2).start()
    o_copy(N - 1).start()
    own_o = pltpu.make_async_copy(o_buf.at[pl.ds(0, TOK)], att.at[:, ds(me * HD, HD)], o_recv.at[0])
    own_o.start()
    relay(3)
    k_move.wait_send()
    v_move.wait_send()
    every("wait_send", q_copy)
    own_o.wait()
    every("wait_recv", o_copy)

    wp_in.wait()
    latent = jnp.dot(att[...], wp[...], preferred_element_type=F32).astype(BF)
    wide = latent.astype(F32)
    lat[0] = latent
    lat_copy = pltpu.make_async_remote_copy(
        src_ref=lat.at[0], dst_ref=lat.at[1], send_sem=b_send.at[0], recv_sem=b_recv.at[0],
        device_id=beside, device_id_type=MESH,
    )
    lat_copy.start()
    for f in range(FRAMES):
        first, last = f * TH * TW, (f + 1) * TH * TW - TW
        edges[pl.ds(f * TW, TW)] = wide[first : first + TW].astype(BF)
        edges[pl.ds((FRAMES + f) * TW, TW)] = wide[last : last + TW].astype(BF)
    for j in range(C // HD):
        lanes = pl.ds(j * HD, HD)
        by_lanes[j] = wide[:, j * HD : (j + 1) * HD]
        edges[pl.ds(64, 32), lanes] = by_lanes[j, pl.ds(0, FRAMES * TH, stride=TW)].astype(BF)
        edges[pl.ds(96, 32), lanes] = by_lanes[j, pl.ds(TW - 1, FRAMES * TH, stride=TW)].astype(BF)
        for n, start in enumerate((0, TW - 1, TW, 2 * TW - 1)):
            corner = by_lanes[j, pl.ds(start, 16, stride=2 * TW)]
            edges[pl.ds(CORNERS + 16 * n, 16), lanes] = corner.astype(BF)

    row, column = me // TILES, lax.rem(me, TILES)

    def rim_rows(n):
        return pl.ds(n * 32, 32) if n < 4 else pl.ds(CORNERS + (n - 4) * 16, 16)

    def rim_copy(n):
        at, size, down, right = RIMS[n]
        to = lax.rem(row + down + TILES, TILES) * TILES + lax.rem(column + right + TILES, TILES)
        return pltpu.make_async_remote_copy(
            src_ref=edges.at[pl.ds(at, size)], dst_ref=rims.at[0, rim_rows(n)],
            send_sem=e_send.at[n], recv_sem=e_recv.at[n],
            device_id={"seq": to}, device_id_type=MESH,
        )

    line = lax.broadcasted_iota(jnp.int32, (8, C), 0)
    stat[...] = jnp.where(
        line == 0,
        jnp.sum(wide, axis=0, keepdims=True),
        jnp.where(line == 1, jnp.sum(wide * wide, axis=0, keepdims=True), 0.0),
    )

    def stat_copy(t):
        return pltpu.make_async_remote_copy(
            src_ref=stat, dst_ref=stats.at[me],
            send_sem=t_send.at[t], recv_sem=t_recv.at[t],
            device_id={"seq": lax.rem(me + t, N)}, device_id_type=MESH,
        )

    every("start", stat_copy)
    for n in range(len(RIMS)):
        rim_copy(n).start()
    stats[me] = stat[...]
    x_t[PLANE:] = jnp.where(
        lax.broadcasted_iota(jnp.int32, (128, TOK), 0) < 3, 1.0, 0.0
    ).astype(BF)
    gain, shift = gain_ref[...], shift_ref[...]
    every("wait_recv", stat_copy)

    size = C // GROUPS
    total = jnp.sum(stats[...], axis=0)
    lane = lax.broadcasted_iota(jnp.int32, (8, C), 1)
    for hop in (1, 2, 4, 8):
        after = pltpu.roll(total, C - hop, 1)
        before = pltpu.roll(total, hop, 1)
        total = total + jnp.where(lax.rem(lane // hop, 2) == 0, after, before)
    total = total / (LEN * size)
    mean = total[0:1]
    var = total[1:2] - mean * mean
    moments[0] = jnp.where(line == 0, mean, jnp.where(line == 1, lax.rsqrt(var + 1e-06), 0.0))

    def to_beside(n, ref):
        return pltpu.make_async_remote_copy(
            src_ref=ref.at[0], dst_ref=ref.at[1], send_sem=b_send.at[n], recv_sem=b_recv.at[n],
            device_id=beside, device_id_type=MESH,
        )

    moments_copy = to_beside(1, moments)
    rims_copy = to_beside(2, rims)
    moments_copy.start()
    for n in range(len(RIMS)):
        rim_copy(n).wait_recv()
    rims_copy.start()

    def decode(which, tile):
        mean, inverse = moments[which, 0:1], moments[which, 1:2]

        def activate(x):
            return jax.nn.silu((x.astype(F32) - mean) * inverse * gain + shift)

        inner = activate(lat[which])
        for f in range(FRAMES):
            for h in range(TH):
                field[f * (TH + 2) + 1 + h, pl.ds(8, TW)] = inner[
                    (f * TH + h) * TW : (f * TH + h + 1) * TW
                ]

        row, column = tile // TILES, lax.rem(tile, TILES)
        above, below = row > 0, row < TILES - 1
        before, after = column > 0, column < TILES - 1
        inside = (
            above, below, before, after,
            above & before, above & after, below & before, below & after,
        )
        for n in range(len(RIMS)):
            rim = jnp.where(inside[n], activate(rims[which, rim_rows(n)]), 0.0)
            for f in range(FRAMES):
                first = f * (TH + 2)
                last = first + TH + 1
                if n < 2:
                    field[last if n else first, pl.ds(8, TW)] = rim[f * TW : (f + 1) * TW]
                elif n < 4:
                    for h in range(TH):
                        k = f * TH + h
                        field[first + h + 1, pl.ds(7 if n == 2 else 16, 1)] = rim[k : k + 1]
                else:
                    k = 4 * f + (3 if n < 6 else 0)
                    side = 7 if n in (4, 6) else 16
                    field[first if n < 6 else last, pl.ds(side, 1)] = rim[k : k + 1]

        def windows(r, carry):
            for s in range(3):
                window = jnp.concatenate(
                    [
                        field[r + (f * (TH + 2) + h), pl.ds(7 + s, TW)]
                        for f in range(FRAMES)
                        for h in range(TH)
                    ],
                    axis=0,
                )
                x_t[ds((r * 3 + s) * C, C)] = jnp.transpose(window.astype(BF))
            return carry

        lax.fori_loop(0, 3, windows, 0)
        if which == 0:
            for i in range(len(pieces)):
                core_copy(i).wait_recv()
        by_frame[2] = jnp.transpose(lat[which, :, ds(x_hi * CH, CH)]).astype(F32) + jnp.dot(
            w_all[:, TAPS * C :], x_t[PLANE:], preferred_element_type=F32
        )
        by_frame[:2] = jnp.zeros((2, CH, TOK), F32)

        def convolve(k, carry):
            x = x_t[ds(k * C, C)]
            for p in range(3):
                by_frame[p] += jnp.dot(
                    w_all[:, pl.ds(pl.multiple_of(p * PLANE + k * C, C), C)], x,
                    preferred_element_type=F32,
                )
            return carry

        lax.fori_loop(0, 9, convolve, 0)
        at = lax.broadcasted_iota(jnp.int32, (CH, TOK), 1)
        frame = TH * TW
        one = jnp.where(at >= frame, pltpu.roll(by_frame[1], frame, 1), 0.0)
        two = jnp.where(at >= 2 * frame, pltpu.roll(by_frame[0], 2 * frame, 1), 0.0)
        out_t[which] = (by_frame[2] + one + two).astype(BF)

    def y_copy(t):
        theirs, hop = t // Z, lax.rem(t, Z)
        video = lax.rem(rep + theirs * Z, N)
        return pltpu.make_async_remote_copy(
            src_ref=out_t.at[theirs, ds(lax.rem(z + hop, Z) * CO, CO)], dst_ref=gathered.at[video],
            send_sem=y_send.at[t], recv_sem=y_recv.at[t],
            device_id={"seq": me + theirs * (twin - me), "rep": along_z(hop)},
            device_id_type=MESH,
        )

    decode(0, me)
    every("start", y_copy, 1, Z)
    gathered[rep] = out_t[0, ds(z * CO, CO)]
    lat_copy.wait_recv()
    moments_copy.wait_recv()
    rims_copy.wait_recv()
    decode(1, twin)
    every("start", y_copy, Z, N)
    for i in range(len(pieces)):
        w_copy(i).wait_send()
        core_copy(i).wait_send()
    for n in range(len(RIMS)):
        rim_copy(n).wait_send()
    lat_copy.wait_send()
    moments_copy.wait_send()
    rims_copy.wait_send()
    every("wait_send", o_copy)
    every("wait_send", stat_copy)
    every("wait_recv", y_copy)
    out_ref[...] = gathered[...]
    every("wait_send", y_copy)


def unit(q, k, v, taps, w_proj, gain, shift, bias):
    sem = pltpu.SemaphoreType.DMA
    vmem = pl.BlockSpec(memory_space=pltpu.VMEM)
    return pl.pallas_call(
        unit_kernel,
        out_shape=jax.ShapeDtypeStruct((N, CO, TOK), BF),
        in_specs=[pl.BlockSpec(memory_space=pl.ANY)] * 5 + [vmem] * 3,
        out_specs=vmem,
        scratch_shapes=[
            pltpu.VMEM((LEN, HD), BF),
            pltpu.VMEM((LEN, HD), BF),
            pltpu.VMEM((LEN, HD), BF),
            pltpu.VMEM((LEN, HD), F32),
            pltpu.VMEM((N, TOK, HD), BF),
            pltpu.VMEM((N, TOK, HD), BF),
            pltpu.VMEM((N, TOK, HD), BF),
            pltpu.VMEM((4, TOK, HD), BF),
            pltpu.VMEM((4, TOK, HD), BF),
            pltpu.VMEM((LEN, HD), BF),
            pltpu.VMEM((LEN, HD), BF),
            pltpu.VMEM((LEN, HD), BF),
            pltpu.VMEM((HD + EXTRA, LEN), BF),
            pltpu.VMEM((LEN, BQ), F32),
            pltpu.VMEM((LEN, BQ), F32),
            pltpu.VMEM((8, BQ), F32),
            pltpu.VMEM((HD, BQ), BF),
            pltpu.VMEM((HD + EXTRA, BQ), F32),
            pltpu.VMEM((LEN, HD), BF),
            pltpu.VMEM((TOK, N * HD), BF),
            pltpu.VMEM((N * HD, C), BF),
            pltpu.VMEM((CH, DEPTH), BF),
            pltpu.VMEM((2, TOK, C), BF),
            pltpu.VMEM((C // HD, TOK, HD), F32),
            pltpu.VMEM((RIM_ROWS, C), BF),
            pltpu.VMEM((2, RIM_ROWS, C), BF),
            pltpu.VMEM((8, C), F32),
            pltpu.VMEM((N, 8, C), F32),
            pltpu.VMEM((2, 8, C), F32),
            pltpu.VMEM((FRAMES * (TH + 2), PITCH, C), F32),
            pltpu.VMEM((PLANE + 128, TOK), BF),
            pltpu.VMEM((3, CH, TOK), F32),
            pltpu.VMEM((2, CH, TOK), BF),
            pltpu.VMEM((N, CO, TOK), BF),
        ]
        + [sem((N,))] * 8
        + [sem((4,))] * 4
        + [sem((4,)), sem((TAPS,))]
        + [sem((7,))] * 4
        + [sem((len(RIMS),))] * 2
        + [sem((N,))] * 2
        + [sem((3,))] * 2
        + [sem((N,))] * 2,
        compiler_params=pltpu.CompilerParams(
            collective_id=0, has_side_effects=True, vmem_limit_bytes=62 * 2**20
        ),
        cost_estimate=pl.CostEstimate(
            flops=4 * LEN * LEN * HD + 2 * TOK * DEPTH * C,
            bytes_accessed=8 * 2**20,
            transcendentals=LEN * LEN,
        ),
        name="unit",
    )(q, k, v, taps, w_proj, gain, shift, bias)


def shards(queries, keys, values, w_proj, norm_gain, norm_bias, conv_weight, conv_bias):
    taps = conv_weight.reshape(TAPS, C, CO).transpose(0, 2, 1)
    q, k, v = (a.reshape(LEN, HD) for a in (queries, keys, values))
    out = unit(
        q, k, v, taps, w_proj, norm_gain[None], norm_bias[None], conv_bias[None]
    )
    return out.transpose(0, 2, 1).reshape(N, 1, FRAMES, TH, TW, CO)


def solution(mesh):
    return jax.shard_map(
        shards,
        mesh=mesh,
        in_specs=(
            P("rep", "seq", None, None),
            P("rep", "seq", None, None),
            P("rep", "seq", None, None),
            P(),
            P(),
            P(),
            P(None, None, None, None, "rep"),
            P("rep"),
        ),
        out_specs=P(None, "seq", None, None, None, "rep"),
        check_vma=False,
    )
```

time: 117 us -> 112 us (0.957)
  Pallas kernels: 114 us -> 109 us
    pallas_call x1, Pallas kernels: 114 us -> 109 us  [unit(): pl.pallas_call(unit_kernel, out_shape=jax.ShapeDtypeStruct((N, CO, TOK),...]
where the time goes in v1:
time: 112 us
  Pallas kernels  109 us (97%)
  local copies, waits for them, and re-layouts  2.27 us (2%)
    pallas_call x1, Pallas kernels, unit(): pl.pallas_call(unit_kernel, out_shape=jax.ShapeDtypeStruct((N, CO, TOK),...  109 us
    transpose x1, local copies, waits for them, and re-layouts, shards(): return out.transpose(0, 2, 1).reshape(N, 1, FRAMES, TH, TW, CO)  2.27 us

profile of v1, /device:TPU:2, one launch (start us, length us, event | category | flops | bytes accessed | tf_op | source)
XLA Modules:
  0.0 111.6 jit_solution(16886042821135201957)
XLA Ops:
  0.0 109.3 %unit.1 = bf16[16,32,256]{2,1,0:T(8,128)(2,1)} custom-call(bf16[4096,128]{1,0:T(8,128)(2,1)} %bitcast.14, bf16[4096,128]{1,0:T(8,128)(2,1)} %bitcast.15, bf16[4096,128]{1,0:T(8,128)(2,1)} %bitcast.16, bf16[27,32,512]{2,1,0:T(8,128)(2,1)} %bitcast.17, bf16[2048,512]{1,0:T(8,128)(2,1)} %wp_ref.1, f32[1,512]{1,0:T(1,128)} %bitcast.18, f32[1,512]{1,0:T(1,128)} %bitcast.19, ...), custom_call_target="tpu_custom_call" | custom-call | flops 12247367680 | bytes 8388608 | tf_op jit(solution)/shard_map/unit/pallas_call | solution.py:576
  109.3 2.3 %copy.10 = bf16[16,256,32]{2,1,0:T(8,128)(2,1)} copy(bf16[16,256,32]{1,2,0:T(8,128)(2,1)} %bitcast.13) | data formatting | bytes 524288 | tf_op jit(solution)/shard_map/transpose | solution.py:643

commit v2 on v1

--- a/solution.py
+++ b/solution.py
@@ -22,7 +22,6 @@
 HALF = CO // 2
 TAPS = 27
 PLANE = 9 * C
-DEPTH = TAPS * C + 128
 BQ = 512
 BK = 512
 EXTRA = 16
@@ -43,10 +42,9 @@
 def unit_kernel(
     q_ref, k_ref, v_ref, taps_ref, wp_ref, gain_ref, shift_ref, bias_ref, out_ref,
     q_raw, k_raw, v_raw, by_token, q_out, k_out, v_out,
-    k_stop, v_stop, q_all, k_all, v_all, v_t, s_even, s_odd, m_buf, q_t, acc, o_buf, att, wp,
-    w_all, lat, by_lanes, edges, rims, stat, stats, moments, field, x_t, by_frame, out_t, gathered,
+    q_all, k_all, v_all, v_t, s_even, s_odd, m_buf, q_t, acc, o_buf, att, wp,
+    w_all, lat, by_lanes, edges, rims, stat, stats, moments, field, ones, by_frame, out_t, gathered,
     q_send, q_recv, k_send, k_recv, v_send, v_recv, o_send, o_recv,
-    k_stop_send, k_stop_recv, v_stop_send, v_stop_recv,
     raw_in, w_own, w_send, w_recv, c_send, c_recv, e_send, e_recv, t_send, t_recv, b_send, b_recv, y_send, y_recv,
 ):
     me = lax.axis_index("seq")
@@ -94,7 +92,9 @@
 
     def own_tap(t):
         return pltpu.make_async_copy(
-            taps_ref.at[t], w_all.at[ds(z * CO, CO), ds(t * C, C)], w_own.at[t]
+            taps_ref.at[t],
+            w_all.at[t // 9, ds(z * CO, CO), ds(lax.rem(t, 9) * C, C)],
+            w_own.at[t],
         )
 
     def tap_start(t, carry):
@@ -113,7 +113,9 @@
     lane = lax.broadcasted_iota(jnp.int32, (CO, HD), 1)
     nought = jnp.zeros((CO, HD), F32)
     parts = jnp.where(lane == 0, high, jnp.where(lane == 1, middle, jnp.where(lane == 2, low, nought)))
-    w_all[ds(z * CO, CO), TAPS * C :] = parts.astype(BF)
+    w_all[0, ds(z * CO, CO), PLANE:] = nought.astype(BF)
+    w_all[1, ds(z * CO, CO), PLANE:] = nought.astype(BF)
+    w_all[2, ds(z * CO, CO), PLANE:] = parts.astype(BF)
     v_t[HD:] = jnp.ones((EXTRA, LEN), BF)
 
     def by_head(copy, raw, out):
@@ -130,72 +132,21 @@
     by_head(k_in, k_raw, k_out)
     pl.semaphore_wait(barrier, N + 2 * (Z - 1))
 
-    band, lo = me // TILES, lax.rem(me // 2, 2)
-
-    def column_of(j):
-        return 2 * (lo + j // 2 - 2 * lo * (j // 2)) + half + j % 2 - 2 * half * (j % 2)
-
-    def across_rows(j, rows):
-        way = -1 if j < 2 else 1
-        return lax.rem(band + way * rows + TILES, TILES) * TILES
-
-    def straight(t):
-        row = lax.rem(me + t, N) // TILES
-        return lax.rem(row - band + TILES, TILES) != 2
-
-    class Exchange:
-        def __init__(self, out, whole, send, recv, stop, stop_send, stop_recv):
-            self.out, self.whole, self.send, self.recv = out, whole, send, recv
-            self.stop, self.stop_send, self.stop_recv = stop, stop_send, stop_recv
-
-        def copy(self, t):
-            to = lax.rem(me + t, N)
-            return pltpu.make_async_remote_copy(
-                src_ref=self.out.at[to], dst_ref=self.whole.at[ds(me * TOK, TOK)],
-                send_sem=self.send.at[t], recv_sem=self.recv.at[t],
-                device_id={"seq": to}, device_id_type=MESH,
-            )
-
-        def first(self, j):
-            to = across_rows(j, 2) + column_of(j)
-            t = lax.rem(to - me + N, N)
-            return pltpu.make_async_remote_copy(
-                src_ref=self.out.at[to], dst_ref=self.stop.at[j],
-                send_sem=self.send.at[t], recv_sem=self.stop_recv.at[j],
-                device_id={"seq": across_rows(j, 1) + lax.rem(me, TILES)}, device_id_type=MESH,
-            )
-
-        def second(self, j):
-            to = across_rows(j, 1) + column_of(j)
-            origin = across_rows(j, -1) + lax.rem(me, TILES)
-            t = lax.rem(to - origin + N, N)
-            return pltpu.make_async_remote_copy(
-                src_ref=self.stop.at[j], dst_ref=self.whole.at[ds(origin * TOK, TOK)],
-                send_sem=self.stop_send.at[j], recv_sem=self.recv.at[t],
-                device_id={"seq": to}, device_id_type=MESH,
-            )
-
-        def start(self):
-            for j in range(4):
-                self.first(j).start()
-
-            def body(t, carry):
-                @pl.when(straight(t))
-                def _():
-                    self.copy(t).start()
-                return carry
-
-            lax.fori_loop(1, N, body, 0)
-
-        def forward(self):
-            for j in range(4):
-                self.first(j).wait_recv()
-                self.second(j).start()
-
-        def wait_send(self):
-            every("wait_send", self.copy)
-            for j in range(4):
-                self.second(j).wait_send()
+    def k_copy(t):
+        to = lax.rem(me + t, N)
+        return pltpu.make_async_remote_copy(
+            src_ref=k_out.at[to], dst_ref=k_all.at[ds(me * TOK, TOK)],
+            send_sem=k_send.at[t], recv_sem=k_recv.at[t],
+            device_id={"seq": to}, device_id_type=MESH,
+        )
+
+    def v_copy(t):
+        to = lax.rem(me + t, N)
+        return pltpu.make_async_remote_copy(
+            src_ref=v_out.at[to], dst_ref=v_all.at[ds(me * TOK, TOK)],
+            send_sem=v_send.at[t], recv_sem=v_recv.at[t],
+            device_id={"seq": to}, device_id_type=MESH,
+        )
 
     def q_copy(t):
         to = lax.rem(me - t + N, N)
@@ -219,9 +170,6 @@
             return carry
         lax.fori_loop(first, last, body, 0)
 
-    k_move = Exchange(k_out, k_all, k_send, k_recv, k_stop, k_stop_send, k_stop_recv)
-    v_move = Exchange(v_out, v_all, v_send, v_recv, v_stop, v_stop_send, v_stop_recv)
-
     pieces = [(-d, 1) for d in (1, 2, 3, 4)] + [(d, -1) for d in (1, 2, 3)]
 
     def shard_rows(d):
@@ -231,7 +179,7 @@
         d, turn = pieces[i]
         held = shard_rows(d + turn)
         return pltpu.make_async_remote_copy(
-            src_ref=w_all.at[held], dst_ref=w_all.at[held],
+            src_ref=w_all.at[:, held], dst_ref=w_all.at[:, held],
             send_sem=w_send.at[i], recv_sem=w_recv.at[i],
             device_id={"rep": along_z(turn)}, device_id_type=MESH,
         )
@@ -239,7 +187,7 @@
     def core_copy(i):
         held = shard_rows(pieces[i][0])
         return pltpu.make_async_remote_copy(
-            src_ref=w_all.at[held], dst_ref=w_all.at[held],
+            src_ref=w_all.at[:, held], dst_ref=w_all.at[:, held],
             send_sem=c_send.at[i], recv_sem=c_recv.at[i],
             device_id={"seq": other_core}, device_id_type=MESH,
         )
@@ -250,13 +198,14 @@
             w_copy(j).start()
         core_copy(i).start()
 
-    k_move.start()
+    every("start", k_copy)
     every("wait", own_tap, 0, TAPS)
     w_copy(0).start()
     w_copy(4).start()
     by_head(v_in, v_raw, v_out)
+    every("start", v_copy)
     by_head(q_in, q_raw, q_out)
-    k_move.forward()
+    every("start", q_copy)
 
     def flip(place, block):
         v_t[:HD, place] = jnp.transpose(block)
@@ -265,9 +214,7 @@
     k_all[mine] = k_out[me]
     flip(mine, v_out[me])
     q_all[:TOK] = q_out[me]
-    every("wait_recv", k_move.copy)
-    v_move.start()
-    every("start", q_copy, 1, 4)
+    every("wait_recv", k_copy)
 
     factor = HD ** (-0.5) * math.log2(math.e)
 
@@ -311,7 +258,7 @@
             weigh(p, keys)
             return top
 
-        top = lax.fori_loop(0, LEN // BK, chunk, lowest)
+        top = lax.fori_loop(0, LEN // BK, chunk, lowest, unroll=2)
         if then is not None:
             settle(top)
         emit(u)
@@ -323,26 +270,20 @@
             0, LEN // BK, lambda c, top: scores(s_even, ds(c * BK, BK), top), lowest
         )
     )
-    v_move.forward()
     relay(0, 1)
     relay(4, 5)
 
     def v_arrive(t, carry):
-        v_move.copy(t).wait_recv()
+        v_copy(t).wait_recv()
         place = ds(lax.rem(me - t + N, N) * TOK, TOK)
         flip(place, v_all[place])
         return carry
 
     lax.fori_loop(1, N, v_arrive, 0)
-    every("start", q_copy, 4, 8)
     relay(1, 2)
     relay(5, 6)
 
     def steps(i, carry):
-        @pl.when(i < 2)
-        def _():
-            every("start", q_copy, 8 + 4 * i, 12 + 4 * i)
-
         step(2 * i, s_even, s_odd)
 
         @pl.when(i > 0)
@@ -355,10 +296,14 @@
         o_copy(4 * i + 2).start()
         o_copy(4 * i + 3).start()
 
-        @pl.when(i == 1)
+        @pl.when(i == 0)
         def _():
             relay(2, 3)
             relay(6)
+
+        @pl.when(i == 2)
+        def _():
+            relay(3)
 
         return carry
 
@@ -371,9 +316,8 @@
     o_copy(N - 1).start()
     own_o = pltpu.make_async_copy(o_buf.at[pl.ds(0, TOK)], att.at[:, ds(me * HD, HD)], o_recv.at[0])
     own_o.start()
-    relay(3)
-    k_move.wait_send()
-    v_move.wait_send()
+    every("wait_send", k_copy)
+    every("wait_send", v_copy)
     every("wait_send", q_copy)
     own_o.wait()
     every("wait_recv", o_copy)
@@ -432,7 +376,7 @@
     for n in range(len(RIMS)):
         rim_copy(n).start()
     stats[me] = stat[...]
-    x_t[PLANE:] = jnp.where(
+    ones[...] = jnp.where(
         lax.broadcasted_iota(jnp.int32, (128, TOK), 0) < 3, 1.0, 0.0
     ).astype(BF)
     gain, shift = gain_ref[...], shift_ref[...]
@@ -499,38 +443,37 @@
                     side = 7 if n in (4, 6) else 16
                     field[first if n < 6 else last, pl.ds(side, 1)] = rim[k : k + 1]
 
-        def windows(r, carry):
-            for s in range(3):
-                window = jnp.concatenate(
-                    [
-                        field[r + (f * (TH + 2) + h), pl.ds(7 + s, TW)]
-                        for f in range(FRAMES)
-                        for h in range(TH)
-                    ],
-                    axis=0,
-                )
-                x_t[ds((r * 3 + s) * C, C)] = jnp.transpose(window.astype(BF))
-            return carry
-
-        lax.fori_loop(0, 3, windows, 0)
         if which == 0:
             for i in range(len(pieces)):
                 core_copy(i).wait_recv()
+        by_frame[:2] = jnp.zeros((2, CH, TOK), F32)
         by_frame[2] = jnp.transpose(lat[which, :, ds(x_hi * CH, CH)]).astype(F32) + jnp.dot(
-            w_all[:, TAPS * C :], x_t[PLANE:], preferred_element_type=F32
-        )
-        by_frame[:2] = jnp.zeros((2, CH, TOK), F32)
-
-        def convolve(k, carry):
-            x = x_t[ds(k * C, C)]
-            for p in range(3):
-                by_frame[p] += jnp.dot(
-                    w_all[:, pl.ds(pl.multiple_of(p * PLANE + k * C, C), C)], x,
-                    preferred_element_type=F32,
-                )
+            w_all[2, :, PLANE:], ones[...], preferred_element_type=F32
+        )
+
+        def convolve(r, carry):
+            x = jnp.concatenate(
+                [
+                    jnp.transpose(
+                        jnp.concatenate(
+                            [
+                                field[r + (f * (TH + 2) + h), pl.ds(7 + s, TW)]
+                                for f in range(FRAMES)
+                                for h in range(TH)
+                            ],
+                            axis=0,
+                        ).astype(BF)
+                    )
+                    for s in range(3)
+                ],
+                axis=0,
+            )
+            w = w_all[:, :, ds(r * 3 * C, 3 * C)].reshape(3 * CH, 3 * C)
+            part = jnp.dot(w, x, preferred_element_type=F32)
+            by_frame[...] += part.reshape(3, CH, TOK)
             return carry
 
-        lax.fori_loop(0, 9, convolve, 0)
+        lax.fori_loop(0, 3, convolve, 0)
         at = lax.broadcasted_iota(jnp.int32, (CH, TOK), 1)
         frame = TH * TW
         one = jnp.where(at >= frame, pltpu.roll(by_frame[1], frame, 1), 0.0)
@@ -586,8 +529,6 @@
             pltpu.VMEM((N, TOK, HD), BF),
             pltpu.VMEM((N, TOK, HD), BF),
             pltpu.VMEM((N, TOK, HD), BF),
-            pltpu.VMEM((4, TOK, HD), BF),
-            pltpu.VMEM((4, TOK, HD), BF),
             pltpu.VMEM((LEN, HD), BF),
             pltpu.VMEM((LEN, HD), BF),
             pltpu.VMEM((LEN, HD), BF),
@@ -600,7 +541,7 @@
             pltpu.VMEM((LEN, HD), BF),
             pltpu.VMEM((TOK, N * HD), BF),
             pltpu.VMEM((N * HD, C), BF),
-            pltpu.VMEM((CH, DEPTH), BF),
+            pltpu.VMEM((3, CH, PLANE + 128), BF),
             pltpu.VMEM((2, TOK, C), BF),
             pltpu.VMEM((C // HD, TOK, HD), F32),
             pltpu.VMEM((RIM_ROWS, C), BF),
@@ -609,13 +550,12 @@
             pltpu.VMEM((N, 8, C), F32),
             pltpu.VMEM((2, 8, C), F32),
             pltpu.VMEM((FRAMES * (TH + 2), PITCH, C), F32),
-            pltpu.VMEM((PLANE + 128, TOK), BF),
+            pltpu.VMEM((128, TOK), BF),
             pltpu.VMEM((3, CH, TOK), F32),
             pltpu.VMEM((2, CH, TOK), BF),
             pltpu.VMEM((N, CO, TOK), BF),
         ]
         + [sem((N,))] * 8
-        + [sem((4,))] * 4
         + [sem((4,)), sem((TAPS,))]
         + [sem((7,))] * 4
         + [sem((len(RIMS),))] * 2
@@ -626,7 +566,7 @@
             collective_id=0, has_side_effects=True, vmem_limit_bytes=62 * 2**20
         ),
         cost_estimate=pl.CostEstimate(
-            flops=4 * LEN * LEN * HD + 2 * TOK * DEPTH * C,
+            flops=4 * LEN * LEN * HD + 2 * TOK * TAPS * C * C,
             bytes_accessed=8 * 2**20,
             transcendentals=LEN * LEN,
         ),

time: 112 us -> 105 us (0.938)
  Pallas kernels: 109 us -> 103 us
    pallas_call x1, Pallas kernels: 109 us -> 103 us  [unit(): pl.pallas_call(unit_kernel, out_shape=jax.ShapeDtypeStruct((N, CO, TOK),...]
where the time goes in v2:
time: 105 us
  Pallas kernels  103 us (98%)
  local copies, waits for them, and re-layouts  2.27 us (2%)
    pallas_call x1, Pallas kernels, unit(): pl.pallas_call(unit_kernel, out_shape=jax.ShapeDtypeStruct((N, CO, TOK),...  103 us
    transpose x1, local copies, waits for them, and re-layouts, shards(): return out.transpose(0, 2, 1).reshape(N, 1, FRAMES, TH, TW, CO)  2.27 us

profile of v2, /device:TPU:2, one launch (start us, length us, event | category | flops | bytes accessed | tf_op | source)
XLA Modules:
  0.0 105.0 jit_solution(11048491848621892985)
XLA Ops:
  0.0 102.7 %unit.1 = bf16[16,32,256]{2,1,0:T(8,128)(2,1)} custom-call(bf16[4096,128]{1,0:T(8,128)(2,1)} %bitcast.14, bf16[4096,128]{1,0:T(8,128)(2,1)} %bitcast.15, bf16[4096,128]{1,0:T(8,128)(2,1)} %bitcast.16, bf16[27,32,512]{2,1,0:T(8,128)(2,1)} %bitcast.17, bf16[2048,512]{1,0:T(8,128)(2,1)} %wp_ref.1, f32[1,512]{1,0:T(1,128)} %bitcast.18, f32[1,512]{1,0:T(1,128)} %bitcast.19, ...), custom_call_target="tpu_custom_call" | custom-call | flops 12213813248 | bytes 8388608 | tf_op jit(solution)/shard_map/unit/pallas_call | solution.py:519
  102.7 2.3 %copy.10 = bf16[16,256,32]{2,1,0:T(8,128)(2,1)} copy(bf16[16,256,32]{1,2,0:T(8,128)(2,1)} %bitcast.13) | data formatting | bytes 524288 | tf_op jit(solution)/shard_map/transpose | solution.py:583

commit v3 on v2

--- a/solution.py
+++ b/solution.py
@@ -23,7 +23,8 @@
 TAPS = 27
 PLANE = 9 * C
 BQ = 512
-BK = 512
+BK = 256
+ROUND = 4
 EXTRA = 16
 STEPS = LEN // BQ
 PITCH = 24
@@ -118,19 +119,26 @@
     w_all[2, ds(z * CO, CO), PLANE:] = parts.astype(BF)
     v_t[HD:] = jnp.ones((EXTRA, LEN), BF)
 
-    def by_head(copy, raw, out):
+    def widen(copy, raw):
         copy.wait()
 
-        def widen(b, carry):
+        def body(b, carry):
             by_token[ds(b * TOK, TOK)] = raw[ds(b * TOK, TOK)].astype(F32)
             return carry
 
-        lax.fori_loop(0, N, widen, 0)
-        for h in range(N):
-            out[h] = by_token[pl.ds(h, TOK, stride=N)].astype(BF)
-
-    by_head(k_in, k_raw, k_out)
-    pl.semaphore_wait(barrier, N + 2 * (Z - 1))
+        lax.fori_loop(0, N, body, 0)
+
+    def head(h):
+        return by_token[pl.ds(h, TOK, stride=N)].astype(BF)
+
+    def leave(out, copy, way):
+        def body(t, carry):
+            to = lax.rem(me + way * t + N, N)
+            out[to] = head(to)
+            copy(t).start()
+            return carry
+
+        lax.fori_loop(1, N, body, 0)
 
     def k_copy(t):
         to = lax.rem(me + t, N)
@@ -198,22 +206,24 @@
             w_copy(j).start()
         core_copy(i).start()
 
-    every("start", k_copy)
+    def flip(place, block):
+        v_t[:HD, place] = jnp.transpose(block)
+
+    mine = ds(me * TOK, TOK)
+    widen(k_in, k_raw)
+    pl.semaphore_wait(barrier, N + 2 * (Z - 1))
+    leave(k_out, k_copy, 1)
+    k_all[mine] = head(me)
     every("wait", own_tap, 0, TAPS)
     w_copy(0).start()
     w_copy(4).start()
-    by_head(v_in, v_raw, v_out)
-    every("start", v_copy)
-    by_head(q_in, q_raw, q_out)
-    every("start", q_copy)
-
-    def flip(place, block):
-        v_t[:HD, place] = jnp.transpose(block)
-
-    mine = ds(me * TOK, TOK)
-    k_all[mine] = k_out[me]
-    flip(mine, v_out[me])
-    q_all[:TOK] = q_out[me]
+    widen(v_in, v_raw)
+    leave(v_out, v_copy, 1)
+    flip(mine, head(me))
+    widen(q_in, q_raw)
+    leave(q_out, q_copy, -1)
+    q_all[:TOK] = head(me)
+
     every("wait_recv", k_copy)
 
     factor = HD ** (-0.5) * math.log2(math.e)
@@ -236,7 +246,7 @@
         return jnp.exp2(below * factor).reshape(BK, BQ).astype(BF)
 
     def weigh(p, keys):
-        acc[...] += jnp.dot(v_t[:, keys], p, preferred_element_type=F32)
+        return jnp.dot(v_t[:, keys], p, preferred_element_type=F32)
 
     def emit(u):
         o = (acc[:HD] / acc[HD : HD + 1]).astype(BF)
@@ -250,15 +260,19 @@
         m = m_buf[...]
         acc[...] = jnp.zeros_like(acc)
 
-        def chunk(c, top):
-            keys = ds(c * BK, BK)
-            p = exps(now, keys, m)
-            if then is not None:
-                top = scores(then, keys, top)
-            weigh(p, keys)
+        def chunks(c, top):
+            total = None
+            for i in range(ROUND):
+                keys = ds((c * ROUND + i) * BK, BK)
+                p = exps(now, keys, m)
+                if then is not None:
+                    top = scores(then, keys, top)
+                got = weigh(p, keys)
+                total = got if total is None else total + got
+            acc[...] += total
             return top
 
-        top = lax.fori_loop(0, LEN // BK, chunk, lowest, unroll=2)
+        top = lax.fori_loop(0, LEN // (ROUND * BK), chunks, lowest)
         if then is not None:
             settle(top)
         emit(u)
@@ -267,7 +281,7 @@
     query_block(0)
     settle(
         lax.fori_loop(
-            0, LEN // BK, lambda c, top: scores(s_even, ds(c * BK, BK), top), lowest
+            0, LEN // BK, lambda c, top: scores(s_even, ds(c * BK, BK), top), lowest, unroll=ROUND
         )
     )
     relay(0, 1)
@@ -316,15 +330,27 @@
     o_copy(N - 1).start()
     own_o = pltpu.make_async_copy(o_buf.at[pl.ds(0, TOK)], att.at[:, ds(me * HD, HD)], o_recv.at[0])
     own_o.start()
-    every("wait_send", k_copy)
-    every("wait_send", v_copy)
-    every("wait_send", q_copy)
     own_o.wait()
     every("wait_recv", o_copy)
 
     wp_in.wait()
     latent = jnp.dot(att[...], wp[...], preferred_element_type=F32).astype(BF)
     wide = latent.astype(F32)
+    line = lax.broadcasted_iota(jnp.int32, (8, C), 0)
+    stat[...] = jnp.where(
+        line == 0,
+        jnp.sum(wide, axis=0, keepdims=True),
+        jnp.where(line == 1, jnp.sum(wide * wide, axis=0, keepdims=True), 0.0),
+    )
+
+    def stat_copy(t):
+        return pltpu.make_async_remote_copy(
+            src_ref=stat, dst_ref=stats.at[me],
+            send_sem=t_send.at[t], recv_sem=t_recv.at[t],
+            device_id={"seq": lax.rem(me + t, N)}, device_id_type=MESH,
+        )
+
+    every("start", stat_copy)
     lat[0] = latent
     lat_copy = pltpu.make_async_remote_copy(
         src_ref=lat.at[0], dst_ref=lat.at[1], send_sem=b_send.at[0], recv_sem=b_recv.at[0],
@@ -358,27 +384,21 @@
             device_id={"seq": to}, device_id_type=MESH,
         )
 
-    line = lax.broadcasted_iota(jnp.int32, (8, C), 0)
-    stat[...] = jnp.where(
-        line == 0,
-        jnp.sum(wide, axis=0, keepdims=True),
-        jnp.where(line == 1, jnp.sum(wide * wide, axis=0, keepdims=True), 0.0),
-    )
-
-    def stat_copy(t):
-        return pltpu.make_async_remote_copy(
-            src_ref=stat, dst_ref=stats.at[me],
-            send_sem=t_send.at[t], recv_sem=t_recv.at[t],
-            device_id={"seq": lax.rem(me + t, N)}, device_id_type=MESH,
-        )
-
-    every("start", stat_copy)
     for n in range(len(RIMS)):
         rim_copy(n).start()
     stats[me] = stat[...]
     ones[...] = jnp.where(
         lax.broadcasted_iota(jnp.int32, (128, TOK), 0) < 3, 1.0, 0.0
     ).astype(BF)
+    for i in range(len(pieces)):
+        core_copy(i).wait_recv()
+
+    def residual(which):
+        by_frame[:2] = jnp.zeros((2, CH, TOK), F32)
+        bias = jnp.dot(w_all[2, :, PLANE:], ones[...], preferred_element_type=F32)
+        by_frame[2] = jnp.transpose(lat[which, :, ds(x_hi * CH, CH)]).astype(F32) + bias
+
+    residual(0)
     gain, shift = gain_ref[...], shift_ref[...]
     every("wait_recv", stat_copy)
 
@@ -443,13 +463,8 @@
                     side = 7 if n in (4, 6) else 16
                     field[first if n < 6 else last, pl.ds(side, 1)] = rim[k : k + 1]
 
-        if which == 0:
-            for i in range(len(pieces)):
-                core_copy(i).wait_recv()
-        by_frame[:2] = jnp.zeros((2, CH, TOK), F32)
-        by_frame[2] = jnp.transpose(lat[which, :, ds(x_hi * CH, CH)]).astype(F32) + jnp.dot(
-            w_all[2, :, PLANE:], ones[...], preferred_element_type=F32
-        )
+        if which:
+            residual(which)
 
         def convolve(r, carry):
             x = jnp.concatenate(
@@ -506,6 +521,9 @@
     lat_copy.wait_send()
     moments_copy.wait_send()
     rims_copy.wait_send()
+    every("wait_send", k_copy)
+    every("wait_send", v_copy)
+    every("wait_send", q_copy)
     every("wait_send", o_copy)
     every("wait_send", stat_copy)
     every("wait_recv", y_copy)

time: 105 us -> 106 us (level)
  no operation moved by 1% of the time
where the time goes in v3:
time: 106 us
  Pallas kernels  103 us (97%)
  local copies, waits for them, and re-layouts  2.27 us (2%)
    pallas_call x1, Pallas kernels, unit(): pl.pallas_call(unit_kernel, out_shape=jax.ShapeDtypeStruct((N, CO, TOK),...  103 us
    transpose x1, local copies, waits for them, and re-layouts, shards(): return out.transpose(0, 2, 1).reshape(N, 1, FRAMES, TH, TW, CO)  2.27 us

profile of v3, /device:TPU:2, one launch (start us, length us, event | category | flops | bytes accessed | tf_op | source)
XLA Modules:
  0.0 105.7 jit_solution(16686728960966782254)
XLA Ops:
  0.0 103.4 %unit.1 = bf16[16,32,256]{2,1,0:T(8,128)(2,1)} custom-call(bf16[4096,128]{1,0:T(8,128)(2,1)} %bitcast.14, bf16[4096,128]{1,0:T(8,128)(2,1)} %bitcast.15, bf16[4096,128]{1,0:T(8,128)(2,1)} %bitcast.16, bf16[27,32,512]{2,1,0:T(8,128)(2,1)} %bitcast.17, bf16[2048,512]{1,0:T(8,128)(2,1)} %wp_ref.1, f32[1,512]{1,0:T(1,128)} %bitcast.18, f32[1,512]{1,0:T(1,128)} %bitcast.19, ...), custom_call_target="tpu_custom_call" | custom-call | flops 12213813248 | bytes 8388608 | tf_op jit(solution)/shard_map/unit/pallas_call | solution.py:537
  103.4 2.3 %copy.10 = bf16[16,256,32]{2,1,0:T(8,128)(2,1)} copy(bf16[16,256,32]{1,2,0:T(8,128)(2,1)} %bitcast.13) | data formatting | bytes 524288 | tf_op jit(solution)/shard_map/transpose | solution.py:601

commit v4 on v3

--- a/solution.py
+++ b/solution.py
@@ -131,14 +131,14 @@
     def head(h):
         return by_token[pl.ds(h, TOK, stride=N)].astype(BF)
 
-    def leave(out, copy, way):
+    def leave(out, copy, way, first=1, last=N):
         def body(t, carry):
             to = lax.rem(me + way * t + N, N)
             out[to] = head(to)
             copy(t).start()
             return carry
 
-        lax.fori_loop(1, N, body, 0)
+        lax.fori_loop(first, last, body, 0)
 
     def k_copy(t):
         to = lax.rem(me + t, N)
@@ -214,14 +214,15 @@
     pl.semaphore_wait(barrier, N + 2 * (Z - 1))
     leave(k_out, k_copy, 1)
     k_all[mine] = head(me)
-    every("wait", own_tap, 0, TAPS)
-    w_copy(0).start()
-    w_copy(4).start()
     widen(v_in, v_raw)
     leave(v_out, v_copy, 1)
     flip(mine, head(me))
     widen(q_in, q_raw)
-    leave(q_out, q_copy, -1)
+    leave(q_out, q_copy, -1, 1, 8)
+    every("wait", own_tap, 0, TAPS)
+    w_copy(0).start()
+    w_copy(4).start()
+    leave(q_out, q_copy, -1, 8, N)
     q_all[:TOK] = head(me)
 
     every("wait_recv", k_copy)
@@ -284,8 +285,6 @@
             0, LEN // BK, lambda c, top: scores(s_even, ds(c * BK, BK), top), lowest, unroll=ROUND
         )
     )
-    relay(0, 1)
-    relay(4, 5)
 
     def v_arrive(t, carry):
         v_copy(t).wait_recv()
@@ -294,8 +293,6 @@
         return carry
 
     lax.fori_loop(1, N, v_arrive, 0)
-    relay(1, 2)
-    relay(5, 6)
 
     def steps(i, carry):
         step(2 * i, s_even, s_odd)
@@ -306,25 +303,27 @@
 
         o_copy(4 * i + 1).start()
 
+        @pl.when(i == 1)
+        def _():
+            relay(0, 1)
+            relay(4, 5)
+
+        @pl.when(i == 2)
+        def _():
+            relay(1, 2)
+            relay(5, 6)
+
         step(2 * i + 1, s_odd, s_even)
         o_copy(4 * i + 2).start()
         o_copy(4 * i + 3).start()
-
-        @pl.when(i == 0)
-        def _():
-            relay(2, 3)
-            relay(6)
-
-        @pl.when(i == 2)
-        def _():
-            relay(3)
-
         return carry
 
     lax.fori_loop(0, STEPS // 2 - 1, steps, 0)
     step(STEPS - 2, s_even, s_odd)
     o_copy(N - 4).start()
     o_copy(N - 3).start()
+    relay(2, 3)
+    relay(6)
     step(STEPS - 1, s_odd, None)
     o_copy(N - 2).start()
     o_copy(N - 1).start()
@@ -390,6 +389,7 @@
     ones[...] = jnp.where(
         lax.broadcasted_iota(jnp.int32, (128, TOK), 0) < 3, 1.0, 0.0
     ).astype(BF)
+    relay(3)
     for i in range(len(pieces)):
         core_copy(i).wait_recv()
 

time: 106 us -> 110 us (1.038)
  Pallas kernels: 103 us -> 107 us
    pallas_call x1, Pallas kernels: 103 us -> 107 us  [unit(): pl.pallas_call(unit_kernel, out_shape=jax.ShapeDtypeStruct((N, CO, TOK),...]
where the time goes in v4:
time: 110 us
  Pallas kernels  107 us (97%)
  local copies, waits for them, and re-layouts  2.27 us (2%)
    pallas_call x1, Pallas kernels, unit(): pl.pallas_call(unit_kernel, out_shape=jax.ShapeDtypeStruct((N, CO, TOK),...  107 us
    transpose x1, local copies, waits for them, and re-layouts, shards(): return out.transpose(0, 2, 1).reshape(N, 1, FRAMES, TH, TW, CO)  2.27 us

profile of v4, /device:TPU:2, one launch (start us, length us, event | category | flops | bytes accessed | tf_op | source)
XLA Modules:
  0.0 109.8 jit_solution(4600804273672363874)
XLA Ops:
  0.0 107.5 %unit.1 = bf16[16,32,256]{2,1,0:T(8,128)(2,1)} custom-call(bf16[4096,128]{1,0:T(8,128)(2,1)} %bitcast.14, bf16[4096,128]{1,0:T(8,128)(2,1)} %bitcast.15, bf16[4096,128]{1,0:T(8,128)(2,1)} %bitcast.16, bf16[27,32,512]{2,1,0:T(8,128)(2,1)} %bitcast.17, bf16[2048,512]{1,0:T(8,128)(2,1)} %wp_ref.1, f32[1,512]{1,0:T(1,128)} %bitcast.18, f32[1,512]{1,0:T(1,128)} %bitcast.19, ...), custom_call_target="tpu_custom_call" | custom-call | flops 12213813248 | bytes 8388608 | tf_op jit(solution)/shard_map/unit/pallas_call | solution.py:537
  107.5 2.3 %copy.10 = bf16[16,256,32]{2,1,0:T(8,128)(2,1)} copy(bf16[16,256,32]{1,2,0:T(8,128)(2,1)} %bitcast.13) | data formatting | bytes 524288 | tf_op jit(solution)/shard_map/transpose | solution.py:601

commit v5 on v2

--- a/solution.py
+++ b/solution.py
@@ -316,15 +316,27 @@
     o_copy(N - 1).start()
     own_o = pltpu.make_async_copy(o_buf.at[pl.ds(0, TOK)], att.at[:, ds(me * HD, HD)], o_recv.at[0])
     own_o.start()
-    every("wait_send", k_copy)
-    every("wait_send", v_copy)
-    every("wait_send", q_copy)
     own_o.wait()
     every("wait_recv", o_copy)
 
     wp_in.wait()
     latent = jnp.dot(att[...], wp[...], preferred_element_type=F32).astype(BF)
     wide = latent.astype(F32)
+    line = lax.broadcasted_iota(jnp.int32, (8, C), 0)
+    stat[...] = jnp.where(
+        line == 0,
+        jnp.sum(wide, axis=0, keepdims=True),
+        jnp.where(line == 1, jnp.sum(wide * wide, axis=0, keepdims=True), 0.0),
+    )
+
+    def stat_copy(t):
+        return pltpu.make_async_remote_copy(
+            src_ref=stat, dst_ref=stats.at[me],
+            send_sem=t_send.at[t], recv_sem=t_recv.at[t],
+            device_id={"seq": lax.rem(me + t, N)}, device_id_type=MESH,
+        )
+
+    every("start", stat_copy)
     lat[0] = latent
     lat_copy = pltpu.make_async_remote_copy(
         src_ref=lat.at[0], dst_ref=lat.at[1], send_sem=b_send.at[0], recv_sem=b_recv.at[0],
@@ -358,21 +370,6 @@
             device_id={"seq": to}, device_id_type=MESH,
         )
 
-    line = lax.broadcasted_iota(jnp.int32, (8, C), 0)
-    stat[...] = jnp.where(
-        line == 0,
-        jnp.sum(wide, axis=0, keepdims=True),
-        jnp.where(line == 1, jnp.sum(wide * wide, axis=0, keepdims=True), 0.0),
-    )
-
-    def stat_copy(t):
-        return pltpu.make_async_remote_copy(
-            src_ref=stat, dst_ref=stats.at[me],
-            send_sem=t_send.at[t], recv_sem=t_recv.at[t],
-            device_id={"seq": lax.rem(me + t, N)}, device_id_type=MESH,
-        )
-
-    every("start", stat_copy)
     for n in range(len(RIMS)):
         rim_copy(n).start()
     stats[me] = stat[...]
@@ -506,6 +503,9 @@
     lat_copy.wait_send()
     moments_copy.wait_send()
     rims_copy.wait_send()
+    every("wait_send", k_copy)
+    every("wait_send", v_copy)
+    every("wait_send", q_copy)
     every("wait_send", o_copy)
     every("wait_send", stat_copy)
     every("wait_recv", y_copy)
@@ -519,7 +519,7 @@
     return pl.pallas_call(
         unit_kernel,
         out_shape=jax.ShapeDtypeStruct((N, CO, TOK), BF),
-        in_specs=[pl.BlockSpec(memory_space=pl.ANY)] * 5 + [vmem] * 3,
+        in_specs=[pl.BlockSpec(memory_space=pltpu.HBM)] * 5 + [vmem] * 3,
         out_specs=vmem,
         scratch_shapes=[
             pltpu.VMEM((LEN, HD), BF),
@@ -563,7 +563,7 @@
         + [sem((3,))] * 2
         + [sem((N,))] * 2,
         compiler_params=pltpu.CompilerParams(
-            collective_id=0, has_side_effects=True, vmem_limit_bytes=62 * 2**20
+            collective_id=0, has_side_effects=True, vmem_limit_bytes=53 * 2**20
         ),
         cost_estimate=pl.CostEstimate(
             flops=4 * LEN * LEN * HD + 2 * TOK * TAPS * C * C,

time: 105 us -> 105 us (level)
  Pallas kernels: 103 us -> 101 us
  local copies, waits for them, and re-layouts: 2.27 us -> 3.33 us
    unnamed x0 -> x6, local copies, waits for them, and re-layouts: none -> 2.02 us
    pallas_call x1, Pallas kernels: 103 us -> 101 us  [unit(): pl.pallas_call(unit_kernel, out_shape=jax.ShapeDtypeStruct((N, CO, TOK),...]
where the time goes in v5:
time: 105 us
  Pallas kernels  101 us (96%)
  local copies, waits for them, and re-layouts  3.33 us (3%)
    pallas_call x1, Pallas kernels, unit(): pl.pallas_call(unit_kernel, out_shape=jax.ShapeDtypeStruct((N, CO, TOK),...  101 us

profile of v5, /device:TPU:2, one launch (start us, length us, event | category | flops | bytes accessed | tf_op | source)
XLA Modules:
  0.0 104.6 jit_solution(17957615267788893665)
XLA Ops:
  0.0 0.0 copy-start
  0.0 0.7 copy-done
  0.7 0.0 copy-start.1
  0.7 0.7 copy-done.1
  1.4 0.0 copy-start.2
  1.4 0.7 copy-done.2
  2.0 101.3 %unit.1 = bf16[16,32,256]{2,1,0:T(8,128)(2,1)S(1)} custom-call(bf16[4096,128]{1,0:T(8,128)(2,1)} %bitcast.17, bf16[4096,128]{1,0:T(8,128)(2,1)} %bitcast.18, bf16[4096,128]{1,0:T(8,128)(2,1)} %bitcast.19, bf16[27,32,512]{2,1,0:T(8,128)(2,1)} %bitcast.20, bf16[2048,512]{1,0:T(8,128)(2,1)} %wp_ref.1, f32[1,512]{1,0:T(1,128)S(1)} %bitcast.14, ...), custom_call_target="tpu_custom_call" | custom-call | flops 12213813248 | bytes 8388608 | tf_op jit(solution)/shard_map/unit/pallas_call | solution.py:519
  103.3 1.3 %copy.10 = bf16[16,256,32]{2,1,0:T(8,128)(2,1)} copy(bf16[16,256,32]{1,2,0:T(8,128)(2,1)S(1)} %bitcast.13) | data formatting | bytes 524288 | tf_op jit(solution)/shard_map/transpose | solution.py:583
Async XLA Ops:
  0.0 0.7 copy-start
  0.7 0.7 copy-start.1
  1.4 0.7 copy-start.2

commit v6 on v5

--- a/solution.py
+++ b/solution.py
@@ -201,9 +201,9 @@
     every("start", k_copy)
     every("wait", own_tap, 0, TAPS)
     w_copy(0).start()
-    w_copy(4).start()
     by_head(v_in, v_raw, v_out)
     every("start", v_copy)
+    w_copy(4).start()
     by_head(q_in, q_raw, q_out)
     every("start", q_copy)
 
@@ -271,7 +271,6 @@
         )
     )
     relay(0, 1)
-    relay(4, 5)
 
     def v_arrive(t, carry):
         v_copy(t).wait_recv()
@@ -281,7 +280,7 @@
 
     lax.fori_loop(1, N, v_arrive, 0)
     relay(1, 2)
-    relay(5, 6)
+    relay(4, 5)
 
     def steps(i, carry):
         step(2 * i, s_even, s_odd)
@@ -299,11 +298,12 @@
         @pl.when(i == 0)
         def _():
             relay(2, 3)
-            relay(6)
+            relay(5, 6)
 
         @pl.when(i == 2)
         def _():
             relay(3)
+            relay(6)
 
         return carry
 
@@ -519,7 +519,7 @@
     return pl.pallas_call(
         unit_kernel,
         out_shape=jax.ShapeDtypeStruct((N, CO, TOK), BF),
-        in_specs=[pl.BlockSpec(memory_space=pltpu.HBM)] * 5 + [vmem] * 3,
+        in_specs=[pl.BlockSpec(memory_space=pl.ANY)] * 5 + [vmem] * 3,
         out_specs=vmem,
         scratch_shapes=[
             pltpu.VMEM((LEN, HD), BF),
@@ -563,7 +563,7 @@
         + [sem((3,))] * 2
         + [sem((N,))] * 2,
         compiler_params=pltpu.CompilerParams(
-            collective_id=0, has_side_effects=True, vmem_limit_bytes=53 * 2**20
+            collective_id=0, has_side_effects=True, vmem_limit_bytes=62 * 2**20
         ),
         cost_estimate=pl.CostEstimate(
             flops=4 * LEN * LEN * HD + 2 * TOK * TAPS * C * C,

time: 105 us -> 105 us (level)
  Pallas kernels: 101 us -> 103 us
  local copies, waits for them, and re-layouts: 3.33 us -> 2.27 us
    unnamed x6 -> x0, local copies, waits for them, and re-layouts: 2.02 us -> none
    pallas_call x1, Pallas kernels: 101 us -> 103 us  [unit(): pl.pallas_call(unit_kernel, out_shape=jax.ShapeDtypeStruct((N, CO, TOK),...]
where the time goes in v6:
time: 105 us
  Pallas kernels  103 us (98%)
  local copies, waits for them, and re-layouts  2.27 us (2%)
    pallas_call x1, Pallas kernels, unit(): pl.pallas_call(unit_kernel, out_shape=jax.ShapeDtypeStruct((N, CO, TOK),...  103 us
    transpose x1, local copies, waits for them, and re-layouts, shards(): return out.transpose(0, 2, 1).reshape(N, 1, FRAMES, TH, TW, CO)  2.27 us

profile of v6, /device:TPU:2, one launch (start us, length us, event | category | flops | bytes accessed | tf_op | source)
XLA Modules:
  0.0 105.3 jit_solution(9507731896367871614)
XLA Ops:
  0.0 103.0 %unit.1 = bf16[16,32,256]{2,1,0:T(8,128)(2,1)} custom-call(bf16[4096,128]{1,0:T(8,128)(2,1)} %bitcast.14, bf16[4096,128]{1,0:T(8,128)(2,1)} %bitcast.15, bf16[4096,128]{1,0:T(8,128)(2,1)} %bitcast.16, bf16[27,32,512]{2,1,0:T(8,128)(2,1)} %bitcast.17, bf16[2048,512]{1,0:T(8,128)(2,1)} %wp_ref.1, f32[1,512]{1,0:T(1,128)} %bitcast.18, f32[1,512]{1,0:T(1,128)} %bitcast.19, ...), custom_call_target="tpu_custom_call" | custom-call | flops 12213813248 | bytes 8388608 | tf_op jit(solution)/shard_map/unit/pallas_call | solution.py:519
  103.0 2.3 %copy.10 = bf16[16,256,32]{2,1,0:T(8,128)(2,1)} copy(bf16[16,256,32]{1,2,0:T(8,128)(2,1)} %bitcast.13) | data formatting | bytes 524288 | tf_op jit(solution)/shard_map/transpose | solution.py:583

commit v7 on v5

--- a/solution.py
+++ b/solution.py
@@ -519,7 +519,7 @@
     return pl.pallas_call(
         unit_kernel,
         out_shape=jax.ShapeDtypeStruct((N, CO, TOK), BF),
-        in_specs=[pl.BlockSpec(memory_space=pltpu.HBM)] * 5 + [vmem] * 3,
+        in_specs=[pl.BlockSpec(memory_space=pl.ANY)] * 5 + [vmem] * 3,
         out_specs=vmem,
         scratch_shapes=[
             pltpu.VMEM((LEN, HD), BF),
@@ -563,7 +563,7 @@
         + [sem((3,))] * 2
         + [sem((N,))] * 2,
         compiler_params=pltpu.CompilerParams(
-            collective_id=0, has_side_effects=True, vmem_limit_bytes=53 * 2**20
+            collective_id=0, has_side_effects=True, vmem_limit_bytes=62 * 2**20
         ),
         cost_estimate=pl.CostEstimate(
             flops=4 * LEN * LEN * HD + 2 * TOK * TAPS * C * C,

time: 105 us -> 105 us (level)
  Pallas kernels: 101 us -> 103 us
  local copies, waits for them, and re-layouts: 3.33 us -> 2.27 us
    unnamed x6 -> x0, local copies, waits for them, and re-layouts: 2.02 us -> none
    pallas_call x1, Pallas kernels: 101 us -> 103 us  [unit(): pl.pallas_call(unit_kernel, out_shape=jax.ShapeDtypeStruct((N, CO, TOK),...]
where the time goes in v7:
time: 105 us
  Pallas kernels  103 us (98%)
  local copies, waits for them, and re-layouts  2.27 us (2%)
    pallas_call x1, Pallas kernels, unit(): pl.pallas_call(unit_kernel, out_shape=jax.ShapeDtypeStruct((N, CO, TOK),...  103 us
    transpose x1, local copies, waits for them, and re-layouts, shards(): return out.transpose(0, 2, 1).reshape(N, 1, FRAMES, TH, TW, CO)  2.27 us

profile of v7, /device:TPU:2, one launch (start us, length us, event | category | flops | bytes accessed | tf_op | source)
XLA Modules:
  0.0 104.9 jit_solution(4748172859077922236)
XLA Ops:
  0.0 102.6 %unit.1 = bf16[16,32,256]{2,1,0:T(8,128)(2,1)} custom-call(bf16[4096,128]{1,0:T(8,128)(2,1)} %bitcast.14, bf16[4096,128]{1,0:T(8,128)(2,1)} %bitcast.15, bf16[4096,128]{1,0:T(8,128)(2,1)} %bitcast.16, bf16[27,32,512]{2,1,0:T(8,128)(2,1)} %bitcast.17, bf16[2048,512]{1,0:T(8,128)(2,1)} %wp_ref.1, f32[1,512]{1,0:T(1,128)} %bitcast.18, f32[1,512]{1,0:T(1,128)} %bitcast.19, ...), custom_call_target="tpu_custom_call" | custom-call | flops 12213813248 | bytes 8388608 | tf_op jit(solution)/shard_map/unit/pallas_call | solution.py:519
  102.6 2.3 %copy.10 = bf16[16,256,32]{2,1,0:T(8,128)(2,1)} copy(bf16[16,256,32]{1,2,0:T(8,128)(2,1)} %bitcast.13) | data formatting | bytes 524288 | tf_op jit(solution)/shard_map/transpose | solution.py:583
